TPU v7x, 32 devices: a whole 2x2x4 slice. The times are simulated.
32 devices in a mesh: ctx: 8 (over z, x), fsdp: 4 (over y, core).
Axes of the slice: x: 2, y: 2, z: 4, core: 2. Of those that a mesh axis runs over, the one named last changes fastest.
Arguments:
- out_grad: bfloat16 [1024, 8192], P('ctx', 'fsdp'), may hold values from -6 to 6
- out_weight: bfloat16 [8192, 8192], P('ctx', 'fsdp'), may hold values from -0.0625 to 0.0625
- projections: bfloat16 [3, 1024, 8192], P(None, 'ctx', 'fsdp'), may hold values from -6 to 6
- short_filters: float32 [3, 3, 8192], P(None, None, 'fsdp'), may hold values from -3 to 3
- residues: float32 [16, 8192], P(None, 'fsdp'), may hold values from -0.06 to 0.06
- decay_rates: float32 [16, 8192], P(None, 'fsdp'), may hold values from 9.765625e-05 to 0.05
Outputs:
- grad_weight: bfloat16 [8192, 8192], P('ctx', 'fsdp')
- grad_projections: bfloat16 [3, 1024, 8192], P(None, 'ctx', 'fsdp')
- grad_short: float32 [3, 3, 8192], P(None, None, 'fsdp')
- grad_residues: float32 [16, 8192], P(None, 'fsdp')
- grad_rates: float32 [16, 8192], P(None, 'fsdp')
All inputs are finite; a program needn't handle non-finite values.
Results may differ from a plain program's by a relative error of at most 0.005.
Values may be sent and summed in bfloat16 or wider, within the bound.
A program may use at most 192 MiB of HBM per device.

v0:
```python
import math

import jax
import jax.numpy as jnp
from jax import lax
from jax.sharding import PartitionSpec as P


def from_behind(block, axis, distance):
    devices = range(lax.axis_size(axis))
    route = [(i - distance, i) for i in devices if i - distance in devices]
    return lax.ppermute(block, axis, route)


def carried_in(array, axis, combine, identity, reverse):
    devices, index = (lax.axis_size(axis), lax.axis_index(axis))
    everything = jax.tree.map(lambda part: lax.all_gather(part, axis), array)
    start = jax.tree.map(
        lambda part, zero: jnp.broadcast_to(jnp.asarray(zero, part.dtype), part.shape),
        array,
        identity,
    )

    def lap(k, before):
        at = devices - 1 - k if reverse else k
        reached = at > index if reverse else at < index
        new = combine(before, jax.tree.map(lambda part: part[at], everything))
        return jax.tree.map(lambda a, b: jnp.where(reached, a, b), new, before)

    return lax.fori_loop(0, devices, lap, start)


def link(earlier, later):
    return (earlier[0] * later[0], later[0] * earlier[1] + later[1])


def local_scan(decay, values):
    length = values.shape[0]
    piece_len = math.gcd(length, 32)
    block_count = length // piece_len
    grouped = values.reshape((block_count, piece_len) + values.shape[1:])
    running = jnp.zeros((block_count,) + decay.shape, jnp.float32)
    outputs = []
    for offset in range(piece_len):
        running = decay * running + grouped[:, offset]
        outputs.append(running)
    inner = jnp.stack(outputs, axis=1)
    jump = jnp.power(decay, float(piece_len))

    def carry_step(carry, final):
        return (jump * carry + final, carry)

    _, entering = lax.scan(carry_step, jnp.zeros(decay.shape, jnp.float32), inner[:, -1])
    steps_in = jnp.arange(piece_len, dtype=jnp.float32) + 1.0
    rising = jnp.power(decay[None], steps_in[:, None, None])
    whole = inner + rising[None] * entering[:, None]
    return whole.reshape((length,) + decay.shape)


def on_device(out_grad, out_weight, projections, short_filters, residues, decay_rates):
    panels = lax.all_gather(out_grad, "fsdp", axis=1, tiled=True)
    length = out_grad.shape[0]
    columns = panels
    grad_y = jnp.dot(
        columns,
        lax.all_gather(out_weight, "ctx", axis=0, tiled=True),
        preferred_element_type=jnp.float32,
    )
    taps = short_filters.shape[1]
    margin = taps - 1
    before = from_behind(projections[:, length - margin :, :], "ctx", 1)
    extended = jnp.concatenate([before, projections], axis=1).astype(jnp.float32)
    branches = short_filters[:, 0, None, :] * extended[:, margin : margin + length, :]
    for offset in range(1, taps):
        branches = (
            branches
            + short_filters[:, offset, None, :]
            * extended[:, margin - offset : margin - offset + length, :]
        )
    q_branch, k_branch, v_branch = (branches[0], branches[1], branches[2])
    product_kv = k_branch * v_branch
    decay = jnp.exp(-decay_rates)
    block_decay = jnp.exp(-decay_rates * float(length))
    positions = jnp.arange(length, dtype=jnp.float32)
    states_local = local_scan(decay, product_kv[:, None, :])
    identity = (jnp.ones_like(decay), jnp.zeros_like(decay))
    state_in = carried_in((block_decay, states_local[-1]), "ctx", link, identity, False)[1]
    rising = jnp.exp(-decay_rates[None] * (positions + 1.0)[:, None, None])
    states = states_local + rising * state_in[None]
    long_out = jnp.sum(residues[None] * states, axis=1)
    y_rounded = (q_branch * long_out).astype(jnp.bfloat16)
    grad_long = grad_y * q_branch
    grad_q = grad_y * long_out
    flipped = jnp.flip(grad_long, axis=0)
    adjoint_local = jnp.flip(local_scan(decay, residues[None] * flipped[:, None, :]), axis=0)
    adjoint_in = carried_in((block_decay, adjoint_local[0]), "ctx", link, identity, True)[1]
    falling = jnp.exp(-decay_rates[None] * (float(length) - positions)[:, None, None])
    adjoint = adjoint_local + falling * adjoint_in[None]
    grad_kv = jnp.sum(adjoint, axis=1)
    grad_res_part = jnp.sum(grad_long[:, None, :] * states, axis=0)
    previous = jnp.concatenate([state_in[None], states[:-1]], axis=0)
    grad_rate_part = -decay * jnp.sum(adjoint * previous, axis=0)
    grad_branches = jnp.stack([grad_q, grad_kv * v_branch, grad_kv * k_branch])
    after = from_behind(grad_branches[:, :margin, :], "ctx", -1)
    extended_back = jnp.concatenate([grad_branches, after], axis=1)
    grad_raw = short_filters[:, 0, None, :] * extended_back[:, 0:length, :]
    filter_terms = [jnp.sum(grad_branches * extended[:, margin : margin + length, :], axis=1)]
    for offset in range(1, taps):
        grad_raw = (
            grad_raw
            + short_filters[:, offset, None, :] * extended_back[:, offset : offset + length, :]
        )
        filter_terms.append(
            jnp.sum(
                grad_branches * extended[:, margin - offset : margin - offset + length, :], axis=1
            )
        )
    filter_part = jnp.stack(filter_terms, axis=1)
    grad_short, grad_res, grad_rate = lax.psum((filter_part, grad_res_part, grad_rate_part), "ctx")
    columns = panels
    grad_weight = lax.psum_scatter(
        lax.dot_general(
            columns, y_rounded, (((0,), (0,)), ((), ())), preferred_element_type=jnp.float32
        ),
        "ctx",
        scatter_dimension=0,
        tiled=True,
    )
    return (
        grad_weight.astype(jnp.bfloat16),
        grad_raw.astype(jnp.bfloat16),
        grad_short,
        grad_res,
        grad_rate,
    )


def solution(mesh):
    placed = (
        P("ctx", "fsdp"),
        P("ctx", "fsdp"),
        P(None, "ctx", "fsdp"),
        P(None, None, "fsdp"),
        P(None, "fsdp"),
        P(None, "fsdp"),
    )
    return jax.shard_map(
        on_device,
        mesh=mesh,
        in_specs=placed,
        out_specs=(
            P("ctx", "fsdp"),
            P(None, "ctx", "fsdp"),
            P(None, None, "fsdp"),
            P(None, "fsdp"),
            P(None, "fsdp"),
        ),
        check_vma=False,
    )
```

profile of v0, /device:TPU:0, one launch (start us, length us, event | category | flops | bytes accessed | tf_op | source)
XLA Modules:
  0.0 2107.3 jit_solution(1541998178786849107)
XLA Ops:
  9.6 4.8 collective-permute-start
  17.3 9.1 broadcast_power_fusion
  43.0 12.3 while.56
  55.3 618.9 %all-gather.11.cloned.1.call-done = bf16[8192,2048]{1,0:T(8,128)(2,1)} async-done(((bf16[1024,2048]{1,0:T(8,128)(2,1)}), bf16[8192,2048]{1,0:T(8,128)(2,1)}) %all-gather.11.cloned.1.call-update) | async-done | bytes 33554448 | tf_op jit(solution)/shard_map/all_gather | solution.py:66
  674.2 17.2 fusion.8
  691.4 6.8 rev.8
  699.0 9.3 broadcast_multiply_fusion
  708.3 6.8 bitcast_add_fusion.4
  786.2 18.9 multiply_add_fusion.1
  810.9 5.7 copy-done.4
  817.5 6.7 copy.25
  824.2 5.8 copy-done.3
  831.5 26.2 %all-gather.7.cloned.1.call-done = f32[8,16,2048]{2,1,0:T(8,128)} async-done(((f32[1,16,2048]{2,1,0:T(8,128)}), f32[8,16,2048]{2,1,0:T(8,128)}) %all-gather.7.cloned.1.call-update) | async-done | bytes 1048592 | tf_op jit(solution)/shard_map/all_gather | solution.py:17
  857.7 8.7 while.57
  866.4 32.8 %all-gather.13.cloned.1.call-done = f32[8,16,2048]{2,1,0:T(8,128)} async-done(((f32[1,16,2048]{2,1,0:T(8,128)}), f32[8,16,2048]{2,1,0:T(8,128)}) %all-gather.13.cloned.1.call-update) | async-done | bytes 1048592 | tf_op jit(solution)/shard_map/all_gather | solution.py:17
  899.2 8.8 while.59
  908.0 14.1 slice_add_fusion
  922.1 14.0 fusion.2
  936.5 8.2 multiply_reduce_fusion
  956.3 23.6 %convolution_bitcast_fusion = f32[8192,2048]{0,1:T(8,128)} fusion(bf16[128,2048]{1,0:T(8,128)(2,1)S(1)} %get-tuple-element.464, bf16[128,8192]{1,0:T(8,128)(2,1)S(1)} %copy-done.12), kind=kOutput, calls=%fused_computation.10 | convolution fusion | flops 4294967296 | bytes 69730304 | tf_op jit(solution)/shard_map/dot_general | solution.py:122
  979.9 47.0 %all-reduce.3.cloned.1.call-done = (f32[3,3,2048]{2,0,1:T(4,128)}, f32[16,2048]{1,0:T(8,128)}, f32[16,2048]{1,0:T(8,128)}) async-done(((f32[3,3,2048]{2,0,1:T(4,128)}, f32[16,2048]{1,0:T(8,128)}, f32[16,2048]{1,0:T(8,128)}), (f32[3,3,2048]{2,0,1:T(4,128)}, f32[16,2048]{1,0:T(8,128)}, f32[16,2048]{1,0:T(8,128)})) %all-reduce.3.cloned.1.call-update) | async-done | bytes 335888 | tf_op jit(solution)/shard_map/psum | solution.py:119
  1028.5 1057.9 %reduce-scatter.2.cloned.1.call-done = f32[1024,2048]{0,1:T(8,128)} async-done(((f32[8192,2048]{0,1:T(8,128)}), f32[1024,2048]{0,1:T(8,128)}) %reduce-scatter.2.cloned.1.call-update) | async-done | bytes 8388624 | tf_op jit(solution)/shard_map/reduce_scatter | solution.py:121
  2086.4 6.1 convert_element_type.14
  2092.5 6.4 copy.27
  (351 shorter events, 145.0 us)
Async XLA Ops:
  7.2 48.1 %all-gather.9.cloned.1.call-start = ((), (), s32[]{:S(2)}) async-start(), calls=%async_computation.2 | async-start | bytes 2621440 | tf_op jit(solution)/shard_map/all_gather | solution.py:61
  7.9 666.3 %all-gather.11.cloned.1.call-start = ((), (), s32[]{:S(2)}) async-start(), calls=%async_computation.4 | async-start | bytes 37748736 | tf_op jit(solution)/shard_map/all_gather | solution.py:66
  8.6 822.8 %all-gather.15.cloned.1.call-start = ((), (), s32[]{:S(2)}) async-start(), calls=%async_computation.6 | async-start | bytes 1179648 | tf_op jit(solution)/shard_map/all_gather | solution.py:17
  9.6 16.9 collective-permute-start
  16.2 841.5 %all-gather.7.cloned.1.call-start = ((), (), s32[]{:S(2)}) async-start(), calls=%async_computation.1 | async-start | bytes 1179648 | tf_op jit(solution)/shard_map/all_gather | solution.py:17
  31.1 660.2 %copy-start.5 = (f32[3,128,2048]{2,1,0:T(8,128)}, f32[3,128,2048]{2,1,0:T(8,128)S(1)}, u32[]{:S(2)}) copy-start(f32[3,128,2048]{2,1,0:T(8,128)S(1)} %multiply_add_fusion.4) | copy-start | bytes 9437188
  751.1 26.6 %copy-start.42 = (f32[4,1,1,2048]{3,0,1,2:T(4,128)S(1)}, f32[4,1,1,2048]{3,0,1,2:T(4,128)}, u32[]{:S(2)}) copy-start(f32[4,1,1,2048]{3,0,1,2:T(4,128)} %copy-done.41) | copy-start | bytes 98308
  751.1 27.6 %copy-start.48 = (f32[4,1,1,2048]{3,0,1,2:T(4,128)S(1)}, f32[4,1,1,2048]{3,0,1,2:T(4,128)}, u32[]{:S(2)}) copy-start(f32[4,1,1,2048]{3,0,1,2:T(4,128)} %copy-done.47) | copy-start | bytes 98308
  752.5 27.3 %copy-start.52 = (f32[4,1,1,2048]{3,0,1,2:T(4,128)S(1)}, f32[4,1,1,2048]{3,0,1,2:T(4,128)}, u32[]{:S(2)}) copy-start(f32[4,1,1,2048]{3,0,1,2:T(4,128)} %copy-done.51) | copy-start | bytes 98308
  752.5 28.4 %copy-start.56 = (f32[4,1,1,2048]{3,0,1,2:T(4,128)S(1)}, f32[4,1,1,2048]{3,0,1,2:T(4,128)}, u32[]{:S(2)}) copy-start(f32[4,1,1,2048]{3,0,1,2:T(4,128)} %copy-done.55) | copy-start | bytes 98308
  753.6 28.4 %copy-start.62 = (f32[4,1,1,2048]{3,0,1,2:T(4,128)S(1)}, f32[4,1,1,2048]{3,0,1,2:T(4,128)}, u32[]{:S(2)}) copy-start(f32[4,1,1,2048]{3,0,1,2:T(4,128)} %copy-done.61) | copy-start | bytes 98308
  754.9 28.2 %copy-start.67 = (f32[4,1,1,2048]{3,0,1,2:T(4,128)S(1)}, f32[4,1,1,2048]{3,0,1,2:T(4,128)}, u32[]{:S(2)}) copy-start(f32[4,1,1,2048]{3,0,1,2:T(4,128)} %copy-done.66) | copy-start | bytes 98308
  756.1 28.5 %copy-start.78 = (f32[4,1,1,2048]{3,0,1,2:T(4,128)S(1)}, f32[4,1,1,2048]{3,0,1,2:T(4,128)}, u32[]{:S(2)}) copy-start(f32[4,1,1,2048]{3,0,1,2:T(4,128)} %copy-done.77) | copy-start | bytes 98308
  756.1 29.7 %copy-start.8 = (f32[16,2048]{1,0:T(8,128)S(1)}, f32[16,2048]{1,0:T(8,128)}, u32[]{:S(2)}) copy-start(f32[16,2048]{1,0:T(8,128)} %get-tuple-element.748) | copy-start | bytes 393220
  756.1 29.7 %copy-start.9 = (f32[16,2048]{1,0:T(8,128)S(1)}, f32[16,2048]{1,0:T(8,128)}, u32[]{:S(2)}) copy-start(f32[16,2048]{1,0:T(8,128)} %custom-call.2) | copy-start | bytes 393220
  817.4 81.8 %all-gather.13.cloned.1.call-start = ((), (), s32[]{:S(2)}) async-start(), calls=%async_computation.5 | async-start | bytes 1179648 | tf_op jit(solution)/shard_map/all_gather | solution.py:17
  817.5 90.4 %copy-start.45 = (f32[16,2048]{1,0:T(8,128)S(1)}, f32[16,2048]{1,0:T(8,128)}, u32[]{:S(2)}) copy-start(f32[16,2048]{1,0:T(8,128)} %get-tuple-element.504) | copy-start | bytes 393220
  831.4 195.5 %all-reduce.3.cloned.1.call-start = ((), (), s32[]{:S(2)}) async-start(), calls=%async_computation.7 | async-start | bytes 720896 | tf_op jit(solution)/shard_map/psum | solution.py:119
  907.9 28.5 %slice-start = ((s8[16777216]{0:T(1024)(128)(4,1)}), s8[4194304]{0:T(1024)(128)(4,1)S(1)}, s32[]{:S(2)}) async-start(s8[16777216]{0:T(1024)(128)(4,1)} %bitcast.363), calls=%async_computation.8 | async-start | bytes 8388608
  908.0 28.5 %slice-start.1 = ((s8[16777216]{0:T(1024)(128)(4,1)}), s8[4194304]{0:T(1024)(128)(4,1)S(1)}, s32[]{:S(2)}) async-start(s8[16777216]{0:T(1024)(128)(4,1)} %bitcast.363), calls=%async_computation.9 | async-start | bytes 8388608
  946.0 6.1 collective-permute-start.1
  956.3 1130.2 %reduce-scatter.2.cloned.1.call-start = ((), (), s32[]{:S(2)}) async-start(), calls=%async_computation.3 | async-start | bytes 75497472 | tf_op jit(solution)/shard_map/reduce_scatter | solution.py:121
  1026.9 1072.0 %copy-start.80 = (f32[16,2048]{1,0:T(8,128)S(1)}, f32[16,2048]{1,0:T(8,128)}, u32[]{:S(2)}) copy-start(f32[16,2048]{1,0:T(8,128)} %get-tuple-element.733) | copy-start | bytes 393220
  1026.9 1072.7 %copy-start.79 = (f32[16,2048]{1,0:T(8,128)S(1)}, f32[16,2048]{1,0:T(8,128)}, u32[]{:S(2)}) copy-start(f32[16,2048]{1,0:T(8,128)} %get-tuple-element.734) | copy-start | bytes 393220
  (70 other events, 967.0 us)
Sparse Core Ops, SparseCore 0:
  9.6 25.2 all-gather.8
  36.4 637.7 all-gather.10
  676.3 40.1 all-gather.14
  817.5 40.1 all-gather.6
  860.2 38.8 all-gather.12
  956.4 70.4 all-reduce.2
  1031.1 1055.2 reduce-scatter.1
where the time goes:
time: 2120 us; the launch traced here: 2110 us
  waiting for transfers between devices  1790 us (84%)
  other arithmetic  196 us (9%)
  local copies, waits for them, and re-layouts  59.2 us (3%)
  matrix products  40.7 us (2%)
    reduce_scatter x1, waiting for transfers between devices, on_device(): lax.psum_scatter(lax.dot_general(columns, y_rounded, (((0,), (0,)), ((),...  1060 us
    all_gather x1, waiting for transfers between devices, on_device(): lax.all_gather(out_weight, 'ctx', axis=0, tiled=True)  619 us
    unnamed x63, other arithmetic  73.4 us
    all_gather x3, waiting for transfers between devices, carried_in(): everything = jax.tree.map(lambda part: lax.all_gather(part, axis), array)  59 us
    psum x1, waiting for transfers between devices, on_device(): lax.psum((filter_part, grad_res_part, grad_rate_part), 'ctx')  47 us
  transfers between devices with their start and end apart: 9, of which 6 were waited for; matrix products, arithmetic and copies ran while one was open for 10% of the time, Pallas kernels for 0%

commit v1 on v0

v1 whole, which is shorter than its diff:
```python
import math

import jax
import jax.numpy as jnp
from jax import lax
from jax.experimental import pallas as pl
from jax.experimental.pallas import tpu as pltpu
from jax.sharding import PartitionSpec as P

CHUNKS = 8
GROUP = 8


def pair_sum(terms):
    while len(terms) > 1:
        paired = [a + b for a, b in zip(terms[0::2], terms[1::2])]
        terms = paired + ([terms[-1]] if len(terms) % 2 else [])
    return terms[0]


def spread(ref, modes, lanes):
    return [jnp.broadcast_to(ref[n], (CHUNKS, lanes)) for n in modes]


def forward_kernel(kv_ref, decay_ref, jump_ref, res_ref, long_ref, entry_ref, final_ref):
    steps, _, lanes = kv_ref.shape
    modes = range(decay_ref.shape[0])
    decay = spread(decay_ref, modes, lanes)
    zeros = [jnp.zeros((CHUNKS, lanes), jnp.float32) for _ in modes]

    def finals(r, state):
        x = kv_ref[r]
        return [d * s + x for d, s in zip(decay, state)]

    state = lax.fori_loop(0, steps, finals, zeros, unroll=4)
    for n in modes:
        final_ref[n] = state[n]
    jump = jump_ref[...]
    entering = jnp.zeros_like(jump)
    for c in range(CHUNKS):
        entry_ref[:, c : c + 1, :] = entering
        entering = jump * entering + final_ref[:, c : c + 1, :]
    res = spread(res_ref, modes, lanes)

    def outputs(r, state):
        x = kv_ref[r]
        state = [d * s + x for d, s in zip(decay, state)]
        long_ref[r] = pair_sum([w * s for w, s in zip(res, state)])
        return state

    lax.fori_loop(0, steps, outputs, [entry_ref[n] for n in modes], unroll=4)


def backward_kernel(
    kv_ref, gl_ref, decay_ref, jump_ref, res_ref, entry_ref,
    gkv_ref, gres_ref, grate_ref, prev_ref, final_ref, enter_ref,
):
    steps, _, lanes = kv_ref.shape
    n_modes = decay_ref.shape[0]
    modes = range(n_modes)
    decay = spread(decay_ref, modes, lanes)
    zeros = [jnp.zeros((CHUNKS, lanes), jnp.float32) for _ in modes]

    def first(r, carry):
        state, adjoint = carry
        x = kv_ref[r]
        g = gl_ref[steps - 1 - r]
        for n in modes:
            prev_ref[r, n] = state[n]
        return (
            [d * s + x for d, s in zip(decay, state)],
            [d * a + g for d, a in zip(decay, adjoint)],
        )

    _, adjoint = lax.fori_loop(0, steps, first, ([entry_ref[n] for n in modes], zeros), unroll=2)
    for n in modes:
        final_ref[n] = adjoint[n]
    jump = jump_ref[...]
    entering = jnp.zeros_like(jump)
    for c in reversed(range(CHUNKS)):
        enter_ref[:, c : c + 1, :] = entering
        entering = jump * entering + final_ref[:, c : c + 1, :]

    for start in range(0, n_modes, GROUP):
        group = range(start, min(start + GROUP, n_modes))
        d_group = spread(decay_ref, group, lanes)
        r_group = spread(res_ref, group, lanes)
        zero = [jnp.zeros((CHUNKS, lanes), jnp.float32) for _ in group]

        def second(k, carry, start=start, group=group, d_group=d_group, r_group=r_group):
            adjoint, res_sum, rate_sum = carry
            r = steps - 1 - k
            g = gl_ref[r]
            x = kv_ref[r]
            adjoint = [d * a + g for d, a in zip(d_group, adjoint)]
            total = pair_sum([w * a for w, a in zip(r_group, adjoint)])
            gkv_ref[r] = total if start == 0 else gkv_ref[r] + total
            res_sum = [s + a * x for s, a in zip(res_sum, adjoint)]
            rate_sum = [s + a * prev_ref[r, n] for s, a, n in zip(rate_sum, adjoint, group)]
            return adjoint, res_sum, rate_sum

        _, res_sum, rate_sum = lax.fori_loop(
            0, steps, second, ([enter_ref[n] for n in group], zero, zero), unroll=2
        )
        for k, n in enumerate(group):
            gres_ref[n] = jnp.sum(res_sum[k], axis=0, keepdims=True)
            grate_ref[n] = (
                -decay_ref[n] * res_ref[n] * jnp.sum(rate_sum[k], axis=0, keepdims=True)
            )


def series_spec(steps, lanes):
    return pl.BlockSpec((steps, CHUNKS, lanes), lambda b: (0, 0, b))


def mode_spec(n_modes, rows, lanes):
    return pl.BlockSpec((n_modes, rows, lanes), lambda b: (0, 0, b))


def run_forward(kv, decay, jump, res):
    steps, _, width = kv.shape
    n_modes = decay.shape[0]
    lanes = math.gcd(width, 128)
    series, row = series_spec(steps, lanes), mode_spec(n_modes, 1, lanes)
    return pl.pallas_call(
        forward_kernel,
        grid=(width // lanes,),
        in_specs=[series, row, row, row],
        out_specs=[series, mode_spec(n_modes, CHUNKS, lanes)],
        out_shape=[
            jax.ShapeDtypeStruct(kv.shape, jnp.float32),
            jax.ShapeDtypeStruct((n_modes, CHUNKS, width), jnp.float32),
        ],
        scratch_shapes=[pltpu.VMEM((n_modes, CHUNKS, lanes), jnp.float32)],
        compiler_params=pltpu.CompilerParams(vmem_limit_bytes=32 * 2**20),
        cost_estimate=pl.CostEstimate(
            flops=6 * kv.size * n_modes, bytes_accessed=8 * kv.size, transcendentals=0
        ),
    )(kv, decay, jump, res)


def run_backward(kv, gl, decay, jump, res, entry):
    steps, _, width = kv.shape
    n_modes = decay.shape[0]
    lanes = math.gcd(width, 128)
    series, row = series_spec(steps, lanes), mode_spec(n_modes, 1, lanes)
    carried = mode_spec(n_modes, CHUNKS, lanes)
    return pl.pallas_call(
        backward_kernel,
        grid=(width // lanes,),
        in_specs=[series, series, row, row, row, carried],
        out_specs=[series, row, row],
        out_shape=[
            jax.ShapeDtypeStruct(kv.shape, jnp.float32),
            jax.ShapeDtypeStruct(decay.shape, jnp.float32),
            jax.ShapeDtypeStruct(decay.shape, jnp.float32),
        ],
        scratch_shapes=[
            pltpu.VMEM((steps, n_modes, CHUNKS, lanes), jnp.float32),
            pltpu.VMEM((n_modes, CHUNKS, lanes), jnp.float32),
            pltpu.VMEM((n_modes, CHUNKS, lanes), jnp.float32),
        ],
        compiler_params=pltpu.CompilerParams(vmem_limit_bytes=44 * 2**20),
        cost_estimate=pl.CostEstimate(
            flops=12 * kv.size * n_modes, bytes_accessed=12 * kv.size, transcendentals=0
        ),
    )(kv, gl, decay, jump, res, entry)


def to_chunks(series):
    length, width = series.shape
    return jnp.swapaxes(series.reshape(CHUNKS, length // CHUNKS, width), 0, 1)


def from_chunks(series):
    steps, _, width = series.shape
    return jnp.swapaxes(series, 0, 1).reshape(CHUNKS * steps, width)


def on_device(out_grad, out_weight, projections, short_filters, residues, decay_rates):
    devices, index = lax.axis_size("ctx"), lax.axis_index("ctx")
    panels = lax.axis_size("fsdp")
    tokens, wide = out_grad.shape
    length = tokens * devices
    share = projections.shape[2] // devices

    series = lax.all_to_all(projections, "ctx", split_axis=2, concat_axis=1, tiled=True)

    rows = tokens // panels
    mine = lax.all_to_all(out_grad, "fsdp", split_axis=0, concat_axis=1, tiled=True)
    mine = lax.all_to_all(mine, "ctx", split_axis=1, concat_axis=0, tiled=True)
    mine = lax.all_gather(mine.reshape(devices, rows, -1), "fsdp", axis=1)
    cotangent = mine.reshape(length, -1)

    def own(array):
        return lax.dynamic_slice_in_dim(array, index * share, share, axis=array.ndim - 1)

    filters, res, rates = own(short_filters), own(residues), own(decay_rates)
    taps = filters.shape[1]
    margin = taps - 1
    steps = length // CHUNKS
    decay = jnp.exp(-rates)[:, None, :]
    jump = jnp.exp(-rates * float(steps))[:, None, :]
    res = res[:, None, :]

    extended = jnp.pad(series, ((0, 0), (margin, 0), (0, 0))).astype(jnp.float32)
    delayed = [extended[:, margin - j : margin - j + length, :] for j in range(taps)]
    branches = sum(filters[:, j, None, :] * delayed[j] for j in range(taps))
    q_branch, k_branch, v_branch = branches[0], branches[1], branches[2]
    kv = to_chunks(k_branch * v_branch)
    long_chunks, entry = run_forward(kv, decay, jump, res)
    long_out = from_chunks(long_chunks)
    y_rounded = (q_branch * long_out).astype(jnp.bfloat16)
    y_all = lax.all_gather(y_rounded, "ctx", axis=1, tiled=True)

    partial = jnp.dot(cotangent, out_weight, preferred_element_type=jnp.float32)
    partial = partial.astype(jnp.bfloat16).reshape(length, devices, share)
    partial = lax.all_to_all(partial, "ctx", split_axis=1, concat_axis=0)
    grad_y = jnp.sum(partial.astype(jnp.float32), axis=0)

    grad_weight = lax.dot_general(
        cotangent, y_all, (((0,), (0,)), ((), ())), preferred_element_type=jnp.float32
    ).astype(jnp.bfloat16)

    gkv_chunks, grad_res, grad_rate = run_backward(
        kv, to_chunks(grad_y * q_branch), decay, jump, res, entry
    )
    grad_kv = from_chunks(gkv_chunks)
    grad_branches = jnp.stack([grad_y * long_out, grad_kv * v_branch, grad_kv * k_branch])
    extended_back = jnp.pad(grad_branches, ((0, 0), (0, margin), (0, 0)))
    grad_raw = sum(
        filters[:, j, None, :] * extended_back[:, j : j + length, :] for j in range(taps)
    ).astype(jnp.bfloat16)
    grad_raw = lax.all_to_all(grad_raw, "ctx", split_axis=1, concat_axis=2, tiled=True)
    grad_short = jnp.stack(
        [jnp.sum(grad_branches * delayed[j], axis=1) for j in range(taps)], axis=1
    )

    n_short, n_modes = 3 * taps, res.shape[0]
    small = jnp.concatenate(
        [grad_short.reshape(n_short, share), grad_res[:, 0, :], grad_rate[:, 0, :]]
    )
    small = lax.all_gather(small, "ctx", axis=1, tiled=True)
    return (
        grad_weight,
        grad_raw,
        small[:n_short].reshape(3, taps, -1),
        small[n_short : n_short + n_modes],
        small[n_short + n_modes :],
    )


def solution(mesh):
    placed = (
        P("ctx", "fsdp"),
        P("ctx", "fsdp"),
        P(None, "ctx", "fsdp"),
        P(None, None, "fsdp"),
        P(None, "fsdp"),
        P(None, "fsdp"),
    )
    return jax.shard_map(
        on_device,
        mesh=mesh,
        in_specs=placed,
        out_specs=(
            P("ctx", "fsdp"),
            P(None, "ctx", "fsdp"),
            P(None, None, "fsdp"),
            P(None, "fsdp"),
            P(None, "fsdp"),
        ),
        check_vma=False,
    )
```

time: 2120 us -> 350 us (0.17)
  waiting for transfers between devices: 1790 us -> 163 us
  other arithmetic: 196 us -> 9.65 us
  blocking collectives: 0 us -> 85.2 us
  matrix products: 40.7 us -> 14.2 us
  local copies, waits for them, and re-layouts: 59.2 us -> 35.6 us
    reduce_scatter x1 -> x0, waiting for transfers between devices: 1060 us -> none  [on_device(): lax.psum_scatter(lax.dot_general(columns, y_rounded, (((0,), (0,)), ((),...]
    all_gather x5 -> x2, waiting for transfers between devices: 678 us -> 14.9 us  [the longest x1 14.9 us: on_device(): mine = lax.all_gather(mine.reshape(devices, rows, -1), 'fsdp', axis=1)]
    all_to_all x0 -> x3, waiting for transfers between devices: none -> 148 us  [the longest x1 127 us: on_device(): partial = lax.all_to_all(partial, 'ctx', split_axis=1, concat_axis=0)]
    unnamed x63 -> x0, other arithmetic: 73.4 us -> none
    all_gather x0 -> x1, blocking collectives: none -> 51.8 us  [on_device(): small = lax.all_gather(small, 'ctx', axis=1, tiled=True)]
    add x16 -> x1, other arithmetic: 49.9 us -> 0.93 us  [on_device(): branches = sum((filters[:, j, None, :] * delayed[j] for j in range(taps)))]
    psum x1 -> x0, waiting for transfers between devices: 47 us -> none  [on_device(): lax.psum((filter_part, grad_res_part, grad_rate_part), 'ctx')]
    all_to_all x0 -> x2, blocking collectives: none -> 33.5 us  [the longest x1 20.4 us: on_device(): mine = lax.all_to_all(mine, 'ctx', split_axis=1, concat_axis=0, tiled=True)]
  transfers between devices with their start and end apart: 9 -> 5, of which waited for: 6 -> 3; matrix products, arithmetic and copies ran while one was open for 10% -> 14% of each run, Pallas kernels for 0% -> 4%
where the time goes in v1:
time: 350 us; the launch traced here: 349 us
  waiting for transfers between devices  163 us (47%)
  blocking collectives  85.2 us (24%)
  local copies, waits for them, and re-layouts  35.6 us (10%)
  between operations  15.8 us (5%)
  matrix products  14.2 us (4%)
  Pallas kernels  13 us (4%)
  starting transfers between devices  12.3 us (4%)
  other arithmetic  9.65 us (3%)
    all_to_all x1, waiting for transfers between devices, on_device(): partial = lax.all_to_all(partial, 'ctx', split_axis=1, concat_axis=0)  127 us
    all_gather x1, blocking collectives, on_device(): small = lax.all_gather(small, 'ctx', axis=1, tiled=True)  51.8 us
    all_to_all x1, waiting for transfers between devices, on_device(): lax.all_to_all(projections, 'ctx', split_axis=2, concat_axis=1, tiled=True)  20.8 us
    all_to_all x1, blocking collectives, on_device(): mine = lax.all_to_all(mine, 'ctx', split_axis=1, concat_axis=0, tiled=True)  20.4 us
    unnamed x26, local copies, waits for them, and re-layouts  15.1 us
    all_gather x1, waiting for transfers between devices, on_device(): mine = lax.all_gather(mine.reshape(devices, rows, -1), 'fsdp', axis=1)  14.9 us
    all_to_all x1, blocking collectives, on_device(): lax.all_to_all(out_grad, 'fsdp', split_axis=0, concat_axis=1, tiled=True)  13.1 us
    dot_general x1, matrix products, on_device(): lax.dot_general(cotangent, y_all, (((0,), (0,)), ((), ())), preferred_ele...  9.43 us
  transfers between devices with their start and end apart: 5, of which 3 were waited for; matrix products, arithmetic and copies ran while one was open for 14% of the time, Pallas kernels for 4%

profile of v1, /device:TPU:0, one launch (start us, length us, event | category | flops | bytes accessed | tf_op | source)
XLA Modules:
  0.0 349.0 jit_solution(17024768496352501107)
XLA Ops:
  8.1 13.1 %all_to_all.77 = bf16[4,32,2048]{2,1,0:T(8,128)(2,1)S(1)} all-to-all(bf16[4,32,2048]{2,1,0:T(8,128)(2,1)} %bitcast.80), channel_id=1, replica_groups=mesh['ctx'=8,'fsdp'=4] {'fsdp'}, dimensions={0} | all-to-all | bytes 1048576 | tf_op jit(solution)/shard_map/all_to_all | solution.py:190
  22.0 20.4 %all_to_all.78 = bf16[32,8,1024]{2,0,1:T(8,128)(2,1)S(1)} all-to-all(bf16[32,8,1024]{2,0,1:T(8,128)(2,1)S(1)} %copy.47), channel_id=1, replica_groups=mesh['ctx'=8,'fsdp'=4] {'ctx'}, dimensions={1} | all-to-all | bytes 1048576 | tf_op jit(solution)/shard_map/all_to_all | solution.py:191
  43.5 2.5 copy.40
  46.0 3.6 %all-to-all-start = ((bf16[3,128,2048]{1,0,2:T(4,128)(2,1)}), bf16[3,128,2048]{1,0,2:T(4,128)(2,1)S(1)}, u32[]{:S(2)}, u32[]{:S(2)}) async-start(bf16[3,128,2048]{1,0,2:T(4,128)(2,1)} %copy.40), calls=%async_computation | async-start | bytes 4194304 | tf_op jit(solution)/shard_map/all_to_all | solution.py:187
  49.7 14.9 %all-gather.6.cloned.1.call-done = bf16[8,128,1024]{2,0,1:T(8,128)(2,1)} async-done(((bf16[8,32,1024]{2,0,1:T(8,128)(2,1)}), bf16[8,128,1024]{2,0,1:T(8,128)(2,1)}) %all-gather.6.cloned.1.call-update) | async-done | bytes 2097168 | tf_op jit(solution)/shard_map/all_gather | solution.py:192
  64.6 2.9 copy.49
  67.5 4.7 %convolution_convert_fusion = bf16[1024,2048]{1,0:T(8,128)(2,1)S(1)} fusion(bf16[1024,1024]{1,0:T(8,128)(2,1)S(1)} %bitcast.76, bf16[1024,2048]{1,0:T(8,128)(2,1)S(1)} %copy-done.8), kind=kOutput, calls=%fused_computation.2 | convolution fusion | flops 4297064448 | bytes 10485760 | tf_op jit(solution)/shard_map/dot_general | solution.py:216
  72.2 1.5 copy.66
  73.7 2.9 copy.50
  76.6 20.8 %all-to-all-done = bf16[3,128,2048]{1,0,2:T(4,128)(2,1)S(1)} async-done(((bf16[3,128,2048]{1,0,2:T(4,128)(2,1)}), bf16[3,128,2048]{1,0,2:T(4,128)(2,1)S(1)}, u32[]{:S(2)}, u32[]{:S(2)}) %all-to-all-start) | async-done | bytes 1572896 | tf_op jit(solution)/shard_map/all_to_all | solution.py:187
  97.4 4.6 %all-to-all-start.3 = ((bf16[1,1024,8,256]{3,1,0,2:T(8,128)(2,1)}), bf16[1,1024,8,256]{3,1,0,2:T(8,128)(2,1)}, u32[]{:S(2)}, u32[]{:S(2)}) async-start(bf16[1,1024,8,256]{3,1,0,2:T(8,128)(2,1)} %copy.50), calls=%async_computation.3 | async-start | bytes 8388608 | tf_op jit(solution)/shard_map/all_to_all | solution.py:218
  105.4 1.7 copy.42
  110.0 4.0 %shard_map.101 = (f32[128,8,256]{2,1,0:T(8,128)S(1)}, f32[16,8,256]{2,1,0:T(8,128)S(1)}) custom-call(f32[128,8,256]{2,1,0:T(8,128)S(1)} %bitcast.61, f32[16,1,256]{2,1,0:T(1,128)S(1)} %copy.44.decay_ref, f32[16,1,256]{2,1,0:T(1,128)S(1)} %broadcast_in_dim.10.jump_ref, f32[16,1,256]{2,1,0:T(1,128)S(1)} %broadcast_in_dim.11.res_ref), custom_call_target="tpu_custom_call" | custom-call | flops 25165824 | bytes 2097152 | tf_op jit(solution)/shard_map/pallas_call | solution.py:125
  115.4 127.4 %all-to-all-done.3 = bf16[1,1024,8,256]{3,1,0,2:T(8,128)(2,1)} async-done(((bf16[1,1024,8,256]{3,1,0,2:T(8,128)(2,1)}), bf16[1,1024,8,256]{3,1,0,2:T(8,128)(2,1)}, u32[]{:S(2)}, u32[]{:S(2)}) %all-to-all-start.3) | async-done | bytes 4194336 | tf_op jit(solution)/shard_map/all_to_all | solution.py:218
  242.9 2.9 convert_reduce_fusion
  246.9 9.0 %shard_map.102 = (f32[128,8,256]{2,1,0:T(8,128)S(1)}, f32[16,1,256]{2,1,0:T(1,128)S(1)}, f32[16,1,256]{2,1,0:T(1,128)S(1)}) custom-call(f32[128,8,256]{2,1,0:T(8,128)S(1)} %bitcast.62, f32[128,8,256]{2,1,0:T(8,128)S(1)} %fusion.1.gl_ref, f32[16,1,256]{2,1,0:T(1,128)S(1)} %copy.44.decay_ref, f32[16,1,256]{2,1,0:T(1,128)S(1)} %broadcast_in_dim.10.jump_ref, ...), custom_call_target="tpu_custom_call" | custom-call | flops 50331648 | bytes 3145728 | tf_op jit(solution)/shard_map/pallas_call | solution.py:148
  256.4 1.4 copy-done.5
  260.9 2.7 copy.56
  263.7 3.8 %all-to-all-start.4 = ((bf16[3,1024,256]{2,0,1:T(4,128)(2,1)}), bf16[3,1024,256]{2,0,1:T(4,128)(2,1)S(1)}, u32[]{:S(2)}, u32[]{:S(2)}) async-start(bf16[3,1024,256]{2,0,1:T(4,128)(2,1)} %copy.56), calls=%async_computation.4 | async-start | bytes 4194304 | tf_op jit(solution)/shard_map/all_to_all | solution.py:234
  267.5 9.4 %convert_bitcast_fusion = bf16[1024,2048]{0,1:T(8,128)(2,1)} fusion(bf16[1024,2048]{1,0:T(8,128)(2,1)} %all-gather.4.cloned.1.call-done, bf16[1024,1024]{1,0:T(8,128)(2,1)} %bitcast.77), kind=kOutput, calls=%fused_computation.1 | convolution fusion | flops 4297064448 | bytes 10485760 | tf_op jit(solution)/shard_map/dot_general | solution.py:221
  277.0 6.4 %copy.59 = bf16[1024,2048]{1,0:T(8,128)(2,1)} copy(bf16[1024,2048]{0,1:T(8,128)(2,1)} %convert_bitcast_fusion) | data formatting | bytes 8388608
  283.5 51.8 %all_gather.11 = f32[41,2048]{1,0:T(8,128)S(1)} all-gather(f32[41,256]{1,0:T(8,128)S(1)} %pad_maximum_fusion.1), channel_id=1, replica_groups=mesh['ctx'=8,'fsdp'=4] {'ctx'}, dimensions={1}, use_global_device_ids=true | all-gather | bytes 377856 | tf_op jit(solution)/shard_map/all_gather | solution.py:243
  338.0 2.0 copy.58
  340.0 1.6 copy.60
  (60 shorter events, 17.2 us)
Async XLA Ops:
  8.0 96.0 %copy-start = (f32[16,2048]{1,0:T(8,128)S(1)}, f32[16,2048]{1,0:T(8,128)}, u32[]{:S(2)}) copy-start(f32[16,2048]{1,0:T(8,128)} %param.10) | copy-start | bytes 393220
  8.0 56.6 %all-gather.6.cloned.1.call-start = ((), (), s32[]{:S(2)}) async-start(), calls=%async_computation.6 | async-start | bytes 2621440 | tf_op jit(solution)/shard_map/all_gather | solution.py:192
  21.2 22.3 %copy-start.7 = (bf16[3,128,2048]{2,1,0:T(8,128)(2,1)S(1)}, bf16[3,128,2048]{2,1,0:T(8,128)(2,1)}, u32[]{:S(2)}) copy-start(bf16[3,128,2048]{2,1,0:T(8,128)(2,1)} %param.8) | copy-start | bytes 4718596
  46.0 51.4 %all-to-all-start = ((bf16[3,128,2048]{1,0,2:T(4,128)(2,1)}), bf16[3,128,2048]{1,0,2:T(4,128)(2,1)S(1)}, u32[]{:S(2)}, u32[]{:S(2)}) async-start(bf16[3,128,2048]{1,0,2:T(4,128)(2,1)} %copy.40), calls=%async_computation | async-start | bytes 4194304 | tf_op jit(solution)/shard_map/all_to_all | solution.py:187
  64.6 2.9 copy-start.8
  67.5 4.8 %copy-start.6 = (bf16[8,128,1024]{2,1,0:T(8,128)(2,1)}, bf16[8,128,1024]{2,1,0:T(8,128)(2,1)S(1)}, u32[]{:S(2)}) copy-start(bf16[8,128,1024]{2,1,0:T(8,128)(2,1)S(1)} %copy.49) | copy-start | bytes 6291460
  97.4 145.5 %all-to-all-start.3 = ((bf16[1,1024,8,256]{3,1,0,2:T(8,128)(2,1)}), bf16[1,1024,8,256]{3,1,0,2:T(8,128)(2,1)}, u32[]{:S(2)}, u32[]{:S(2)}) async-start(bf16[1,1024,8,256]{3,1,0,2:T(8,128)(2,1)} %copy.50), calls=%async_computation.3 | async-start | bytes 8388608 | tf_op jit(solution)/shard_map/all_to_all | solution.py:218
  102.0 165.5 %all-gather.4.cloned.1.call-start = ((), (), s32[]{:S(2)}) async-start(), calls=%async_computation.5 | async-start | bytes 4718592 | tf_op jit(solution)/shard_map/all_gather | solution.py:214
  107.4 1.7 copy-start.2
  109.2 5.2 %copy-start.4 = (f32[3,1024,256]{2,1,0:T(8,128)}, f32[3,1024,256]{2,1,0:T(8,128)S(1)}, u32[]{:S(2)}) copy-start(f32[3,1024,256]{2,1,0:T(8,128)S(1)} %multiply_add_fusion) | copy-start | bytes 9437188
  255.9 1.9 copy-start.5
  256.4 2.5 copy-start.3
  263.7 73.0 %all-to-all-start.4 = ((bf16[3,1024,256]{2,0,1:T(4,128)(2,1)}), bf16[3,1024,256]{2,0,1:T(4,128)(2,1)S(1)}, u32[]{:S(2)}, u32[]{:S(2)}) async-start(bf16[3,1024,256]{2,0,1:T(4,128)(2,1)} %copy.56), calls=%async_computation.4 | async-start | bytes 4194304 | tf_op jit(solution)/shard_map/all_to_all | solution.py:234
  338.0 3.5 %copy-start.1 = (f32[16,2048]{1,0:T(8,128)S(1)}, f32[16,2048]{1,0:T(8,128)}, u32[]{:S(2)}) copy-start(f32[16,2048]{1,0:T(8,128)} %param.10) | copy-start | bytes 393220
Sparse Core Ops, SparseCore 0:
  43.6 20.9 all-gather.5
Sparse Core Ops, SparseCore 1:
  115.5 129.8 all-gather.3

commit v2 on v1

--- a/solution.py
+++ b/solution.py
@@ -213,10 +213,27 @@
     y_rounded = (q_branch * long_out).astype(jnp.bfloat16)
     y_all = lax.all_gather(y_rounded, "ctx", axis=1, tiled=True)
 
-    partial = jnp.dot(cotangent, out_weight, preferred_element_type=jnp.float32)
-    partial = partial.astype(jnp.bfloat16).reshape(length, devices, share)
-    partial = lax.all_to_all(partial, "ctx", split_axis=1, concat_axis=0)
-    grad_y = jnp.sum(partial.astype(jnp.float32), axis=0)
+    outer, side = devices // 2, lax.rem(index, 2)
+    paired = out_weight.reshape(out_weight.shape[0], outer, 2, share)
+
+    def half(which):
+        columns = lax.dynamic_index_in_dim(paired, which, axis=2, keepdims=False)
+        return columns.reshape(-1, outer * share)
+
+    swap = [(i, i ^ 1) for i in range(devices)]
+    lanes_of = [[2 * z + x for z in range(outer)] for x in range(2)]
+    theirs, ours = half(1 - side), half(side)
+    pieces = []
+    for piece in jnp.split(cotangent, 2, axis=0):
+        sent = jnp.dot(piece, theirs, preferred_element_type=jnp.float32)
+        other = lax.ppermute(sent.astype(jnp.bfloat16), "ctx", swap)
+        kept = jnp.dot(piece, ours, preferred_element_type=jnp.float32)
+        both = (kept + other.astype(jnp.float32)).astype(jnp.bfloat16)
+        terms = lax.all_to_all(
+            both.reshape(-1, outer, share), "ctx", 1, 0, axis_index_groups=lanes_of
+        )
+        pieces.append(jnp.sum(terms.astype(jnp.float32), axis=0))
+    grad_y = jnp.concatenate(pieces, axis=0)
 
     grad_weight = lax.dot_general(
         cotangent, y_all, (((0,), (0,)), ((), ())), preferred_element_type=jnp.float32
@@ -231,7 +248,6 @@
     grad_raw = sum(
         filters[:, j, None, :] * extended_back[:, j : j + length, :] for j in range(taps)
     ).astype(jnp.bfloat16)
-    grad_raw = lax.all_to_all(grad_raw, "ctx", split_axis=1, concat_axis=2, tiled=True)
     grad_short = jnp.stack(
         [jnp.sum(grad_branches * delayed[j], axis=1) for j in range(taps)], axis=1
     )
@@ -240,13 +256,31 @@
     small = jnp.concatenate(
         [grad_short.reshape(n_short, share), grad_res[:, 0, :], grad_rate[:, 0, :]]
     )
-    small = lax.all_gather(small, "ctx", axis=1, tiled=True)
+    small = jnp.pad(small, ((0, -small.shape[0] % 16), (0, 0)))
+    padded = small.shape[0]
+    high = lax.reduce_precision(small, 8, 7)
+    parts = jnp.concatenate([high, small - high]).astype(jnp.bfloat16)
+    own_rows = 3 * tokens
+    sent = jnp.swapaxes(grad_raw.reshape(3, devices, tokens, share), 0, 1)
+    sent = jnp.concatenate(
+        [
+            sent.reshape(devices, own_rows, share),
+            jnp.broadcast_to(parts[None], (devices,) + parts.shape),
+        ],
+        axis=1,
+    )
+    got = lax.all_to_all(sent, "ctx", 0, 0)
+    grad_raw = got[:, :own_rows].reshape(devices, 3, tokens, share)
+    grad_raw = jnp.transpose(grad_raw, (1, 2, 0, 3)).reshape(3, tokens, -1)
+    low = got[:, own_rows + padded :].astype(jnp.float32)
+    small = got[:, own_rows : own_rows + padded].astype(jnp.float32) + low
+    small = jnp.swapaxes(small, 0, 1).reshape(padded, -1)
     return (
         grad_weight,
         grad_raw,
         small[:n_short].reshape(3, taps, -1),
         small[n_short : n_short + n_modes],
-        small[n_short + n_modes :],
+        small[n_short + n_modes : n_short + 2 * n_modes],
     )
 
 

time: 350 us -> 283 us (0.81)
  waiting for transfers between devices: 163 us -> 94.2 us
  blocking collectives: 85.2 us -> 33.5 us
  other arithmetic: 9.65 us -> 30.2 us
  local copies, waits for them, and re-layouts: 35.6 us -> 53.8 us
  starting transfers between devices: 12.3 us -> 19.9 us
  matrix products: 14.2 us -> 20.9 us
    all_to_all x2 -> x3, waiting for transfers between devices: 127 us -> 67.7 us  [the longest x2 38.4 us: on_device(): lax.all_to_all(both.reshape(-1, outer, share), 'ctx', 1, 0, axis_index_gr...]
    all_gather x1 -> x0, blocking collectives: 51.8 us -> none  [on_device(): small = lax.all_gather(small, 'ctx', axis=1, tiled=True)]
    all_gather x1, waiting for transfers between devices: 14.9 us -> 2.85 us  [on_device(): mine = lax.all_gather(mine.reshape(devices, rows, -1), 'fsdp', axis=1)]
    dot_general x1 -> x4, matrix products: 4.73 us -> 12.5 us  [the longest x2 7.98 us: on_device(): kept = jnp.dot(piece, ours, preferred_element_type=jnp.float32)]
    reshape x0 -> x4, local copies, waits for them, and re-layouts: none -> 5.57 us  [the longest x3 4.22 us: from_chunks(): return jnp.swapaxes(series, 0, 1).reshape(CHUNKS * steps, width)]
    add x1, other arithmetic: 0.93 us -> 5.78 us  [on_device(): branches = sum((filters[:, j, None, :] * delayed[j] for j in range(taps)))]
    all_to_all x2 -> x3, starting transfers between devices: 8.38 us -> 13.1 us  [the longest x2 8.52 us: on_device(): lax.all_to_all(both.reshape(-1, outer, share), 'ctx', 1, 0, axis_index_gr...]
    unnamed x26 -> x34, local copies, waits for them, and re-layouts: 15.1 us -> 19.8 us
  transfers between devices with their start and end apart: 5 -> 8, of which waited for: 3 -> 6; matrix products, arithmetic and copies ran while one was open for 14% -> 33% of each run, Pallas kernels for 4% -> 5%
where the time goes in v2:
time: 283 us; the launch traced here: 281 us
  waiting for transfers between devices  94.2 us (33%)
  local copies, waits for them, and re-layouts  53.8 us (19%)
  blocking collectives  33.5 us (12%)
  other arithmetic  30.2 us (11%)
  matrix products  20.9 us (7%)
  starting transfers between devices  19.9 us (7%)
  between operations  15.9 us (6%)
  Pallas kernels  13 us (5%)
    all_to_all x2, waiting for transfers between devices, on_device(): lax.all_to_all(both.reshape(-1, outer, share), 'ctx', 1, 0, axis_index_gr...  38.4 us
    all_to_all x1, waiting for transfers between devices, on_device(): got = lax.all_to_all(sent, 'ctx', 0, 0)  29.3 us
    all_to_all x1, waiting for transfers between devices, on_device(): lax.all_to_all(projections, 'ctx', split_axis=2, concat_axis=1, tiled=True)  22.4 us
    all_to_all x1, blocking collectives, on_device(): mine = lax.all_to_all(mine, 'ctx', split_axis=1, concat_axis=0, tiled=True)  20.4 us
    unnamed x34, local copies, waits for them, and re-layouts  19.8 us
    all_to_all x1, blocking collectives, on_device(): lax.all_to_all(out_grad, 'fsdp', split_axis=0, concat_axis=1, tiled=True)  13.1 us
    pallas_call x1, Pallas kernels, run_backward(): pl.pallas_call(backward_kernel, grid=(width // lanes,), in_specs=[series,...  8.96 us
    all_to_all x2, starting transfers between devices, on_device(): lax.all_to_all(both.reshape(-1, outer, share), 'ctx', 1, 0, axis_index_gr...  8.52 us
  transfers between devices with their start and end apart: 8, of which 6 were waited for; matrix products, arithmetic and copies ran while one was open for 33% of the time, Pallas kernels for 5%

profile of v2, /device:TPU:0, one launch (start us, length us, event | category | flops | bytes accessed | tf_op | source)
XLA Modules:
  0.0 281.4 jit_solution(369659426919366264)
XLA Ops:
  8.0 13.1 %all_to_all.73 = bf16[4,32,2048]{2,1,0:T(8,128)(2,1)S(1)} all-to-all(bf16[4,32,2048]{2,1,0:T(8,128)(2,1)} %bitcast.131), channel_id=1, replica_groups=mesh['ctx'=8,'fsdp'=4] {'fsdp'}, dimensions={0} | all-to-all | bytes 1048576 | tf_op jit(solution)/shard_map/all_to_all | solution.py:190
  22.0 20.4 %all_to_all.74 = bf16[32,8,1024]{2,0,1:T(8,128)(2,1)S(1)} all-to-all(bf16[32,8,1024]{2,0,1:T(8,128)(2,1)S(1)} %copy.76), channel_id=1, replica_groups=mesh['ctx'=8,'fsdp'=4] {'ctx'}, dimensions={1} | all-to-all | bytes 1048576 | tf_op jit(solution)/shard_map/all_to_all | solution.py:191
  46.0 3.6 %all-to-all-start = ((bf16[3,128,2048]{1,0,2:T(4,128)(2,1)}), bf16[3,128,2048]{1,0,2:T(4,128)(2,1)S(1)}, u32[]{:S(2)}, u32[]{:S(2)}) async-start(bf16[3,128,2048]{1,0,2:T(4,128)(2,1)} %copy.66), calls=%async_computation | async-start | bytes 4194304 | tf_op jit(solution)/shard_map/all_to_all | solution.py:187
  49.6 6.5 %copy.79 = bf16[1024,2048]{0,1:T(8,128)(2,1)} copy(bf16[1024,2048]{1,0:T(8,128)(2,1)} %param.7) | data formatting | bytes 8388608 | tf_op args[1]
  57.0 4.7 %constant_dynamic-slice_fusion.3 = (bf16[1024,4,1,256]{0,3,2,1:T(8,128)(2,1)}, bf16[1024,4,1,256]{0,3,2,1:T(8,128)(2,1)}) fusion(bf16[1024,4,2,256]{0,3,2,1:T(8,128)(2,1)} %bitcast.104, s32[]{:T(128)S(6)} %select_n.13, s32[]{:T(128)S(6)} %select_n.14), kind=kLoop, calls=%fused_computation.57 | loop fusion | bytes 8388616 | tf_op jit(solution)/shard_map/jit(dynamic_index_in_dim)/dynamic_slice | solution.py:220
  61.7 2.9 %all-gather.6.cloned.1.call-done = bf16[8,128,1024]{2,0,1:T(8,128)(2,1)} async-done(((bf16[8,32,1024]{2,0,1:T(8,128)(2,1)}), bf16[8,128,1024]{2,0,1:T(8,128)(2,1)}) %all-gather.6.cloned.1.call-update) | async-done | bytes 2097168 | tf_op jit(solution)/shard_map/all_gather | solution.py:192
  64.6 2.7 copy.78
  75.0 22.4 %all-to-all-done = bf16[3,128,2048]{1,0,2:T(4,128)(2,1)S(1)} async-done(((bf16[3,128,2048]{1,0,2:T(4,128)(2,1)}), bf16[3,128,2048]{1,0,2:T(4,128)(2,1)S(1)}, u32[]{:S(2)}, u32[]{:S(2)}) %all-to-all-start) | async-done | bytes 1572896 | tf_op jit(solution)/shard_map/all_to_all | solution.py:187
  101.4 2.6 pad_convert_fusion
  107.8 3.5 %fusion.6 = bf16[512,1024]{0,1:T(8,128)(2,1)} fusion(bf16[512,1024]{0,1:T(8,128)(2,1)} %collective-permute-done, bf16[1024,1024]{0,1:T(8,128)(2,1)S(1)} %bitcast.120, bf16[512,1024]{1,0:T(8,128)(2,1)S(1)} %bitcast.130), kind=kOutput, calls=%fused_computation.18 | convolution fusion | flops 1075314688 | bytes 5242880 | tf_op jit(solution)/shard_map/dot_general | solution.py:230
  111.3 4.3 %all-to-all-start.3 = ((bf16[1,512,4,256]{1,3,0,2:T(8,128)(2,1)}), bf16[1,512,4,256]{1,3,0,2:T(8,128)(2,1)}, u32[]{:S(2)}, u32[]{:S(2)}) async-start(bf16[1,512,4,256]{1,3,0,2:T(8,128)(2,1)} %bitcast.21), calls=%async_computation.3 | async-start | bytes 2097152 | tf_op jit(solution)/shard_map/all_to_all | solution.py:232
  115.8 5.8 %multiply_add_fusion = f32[3,1024,256]{1,2,0:T(8,128)S(1)} fusion(f32[3,1026,256]{1,2,0:T(8,128)} %pad_convert_fusion, f32[3,256]{1,0:T(4,128)S(1)} %get-tuple-element.62, f32[3,256]{1,0:T(4,128)S(1)} %get-tuple-element.63, f32[3,256]{1,0:T(4,128)S(1)} %bitcast.136), kind=kLoop, calls=%fused_computation.12 | loop fusion | flops 3932160 | bytes 12592128 | tf_op jit(solution)/shard_map/add | solution.py:208
  124.5 4.0 %shard_map.101 = (f32[128,8,256]{2,1,0:T(8,128)S(1)}, f32[16,8,256]{2,1,0:T(8,128)S(1)}) custom-call(f32[128,8,256]{2,1,0:T(8,128)S(1)} %bitcast.100, f32[16,1,256]{2,1,0:T(1,128)S(1)} %copy.72.decay_ref, f32[16,1,256]{2,1,0:T(1,128)S(1)} %broadcast_in_dim.16.jump_ref, f32[16,1,256]{2,1,0:T(1,128)S(1)} %broadcast_in_dim.17.res_ref), custom_call_target="tpu_custom_call" | custom-call | flops 25165824 | bytes 2097152 | tf_op jit(solution)/shard_map/pallas_call | solution.py:125
  132.7 4.4 %fusion.5 = bf16[512,1024]{0,1:T(8,128)(2,1)} fusion(bf16[512,1024]{0,1:T(8,128)(2,1)} %collective-permute-done.1, bf16[1024,1024]{0,1:T(8,128)(2,1)} %bitcast.119, bf16[512,1024]{1,0:T(8,128)(2,1)} %bitcast.127), kind=kOutput, calls=%fused_computation.16 | convolution fusion | flops 1075314688 | bytes 5242880 | tf_op jit(solution)/shard_map/dot_general | solution.py:230
  137.1 3.5 %all-to-all-done.3 = bf16[1,512,4,256]{1,3,0,2:T(8,128)(2,1)} async-done(((bf16[1,512,4,256]{1,3,0,2:T(8,128)(2,1)}), bf16[1,512,4,256]{1,3,0,2:T(8,128)(2,1)}, u32[]{:S(2)}, u32[]{:S(2)}) %all-to-all-start.3) | async-done | bytes 1048608 | tf_op jit(solution)/shard_map/all_to_all | solution.py:232
  140.6 4.2 %all-to-all-start.4 = ((bf16[1,512,4,256]{1,3,0,2:T(8,128)(2,1)}), bf16[1,512,4,256]{1,3,0,2:T(8,128)(2,1)}, u32[]{:S(2)}, u32[]{:S(2)}) async-start(bf16[1,512,4,256]{1,3,0,2:T(8,128)(2,1)} %bitcast.126), calls=%async_computation.4 | async-start | bytes 2097152 | tf_op jit(solution)/shard_map/all_to_all | solution.py:232
  148.9 34.9 %all-to-all-done.4 = bf16[1,512,4,256]{1,3,0,2:T(8,128)(2,1)} async-done(((bf16[1,512,4,256]{1,3,0,2:T(8,128)(2,1)}), bf16[1,512,4,256]{1,3,0,2:T(8,128)(2,1)}, u32[]{:S(2)}, u32[]{:S(2)}) %all-to-all-start.4) | async-done | bytes 1048608 | tf_op jit(solution)/shard_map/all_to_all | solution.py:232
  191.6 9.0 %shard_map.102 = (f32[128,8,256]{2,1,0:T(8,128)S(1)}, f32[16,1,256]{2,1,0:T(1,128)S(1)}, f32[16,1,256]{2,1,0:T(1,128)S(1)}) custom-call(f32[128,8,256]{2,1,0:T(8,128)S(1)} %bitcast.101, f32[128,8,256]{2,1,0:T(8,128)S(1)} %fusion.10.gl_ref, f32[16,1,256]{2,1,0:T(1,128)S(1)} %copy.72.decay_ref, f32[16,1,256]{2,1,0:T(1,128)S(1)} %broadcast_in_dim.16.jump_ref, ...), custom_call_target="tpu_custom_call" | custom-call | flops 50331648 | bytes 3145728 | tf_op jit(solution)/shard_map/pallas_call | solution.py:148
  208.7 3.1 %fusion.3 = bf16[3,1024,256]{1,2,0:T(8,128)(2,1)} fusion(f32[3,1024,256]{1,2,0:T(8,128)S(1)} %get-tuple-element.47, f32[3,256]{1,0:T(4,128)S(1)} %get-tuple-element.62, f32[3,256]{1,0:T(4,128)S(1)} %get-tuple-element.63, f32[3,256]{1,0:T(4,128)S(1)} %bitcast.137), kind=kLoop, calls=%fused_computation.6 | loop fusion | flops 4718592 | bytes 4727808 | tf_op jit(solution)/shard_map/convert_element_type | solution.py:250
  215.0 3.1 %pad_maximum_fusion.1 = bf16[8,480,256]{2,1,0:T(8,128)(2,1)} fusion(bf16[8,96,256]{2,1,0:T(8,128)(2,1)S(1)} %broadcast_in_dim.18, bf16[8,384,256]{2,1,0:T(8,128)(2,1)} %bitcast.112), kind=kLoop, calls=%fused_computation.19 | loop fusion | flops 3932160 | bytes 3932160 | tf_op jit(solution)/shard_map/concatenate | solution.py:265
  218.0 4.5 %all-to-all-start.5 = ((bf16[8,480,256]{2,1,0:T(8,128)(2,1)}), bf16[8,480,256]{2,1,0:T(8,128)(2,1)}, u32[]{:S(2)}, u32[]{:S(2)}) async-start(bf16[8,480,256]{2,1,0:T(8,128)(2,1)} %pad_maximum_fusion.1), calls=%async_computation.5 | async-start | bytes 3932160 | tf_op jit(solution)/shard_map/all_to_all | solution.py:272
  223.8 8.4 %convert_bitcast_fusion = bf16[1024,2048]{0,1:T(8,128)(2,1)} fusion(bf16[1024,2048]{0,1:T(8,128)(2,1)} %all-gather.4.cloned.1.call-done, bf16[1024,1024]{1,0:T(8,128)(2,1)S(1)} %bitcast.107), kind=kOutput, calls=%fused_computation | convolution fusion | flops 4297064448 | bytes 10485760 | tf_op jit(solution)/shard_map/dot_general | solution.py:238
  232.2 6.4 %copy.102 = bf16[1024,2048]{1,0:T(8,128)(2,1)} copy(bf16[1024,2048]{0,1:T(8,128)(2,1)} %convert_bitcast_fusion) | data formatting | bytes 8388608
  238.6 29.3 %all-to-all-done.5 = bf16[8,480,256]{2,1,0:T(8,128)(2,1)} async-done(((bf16[8,480,256]{2,1,0:T(8,128)(2,1)}), bf16[8,480,256]{2,1,0:T(8,128)(2,1)}, u32[]{:S(2)}, u32[]{:S(2)}) %all-to-all-start.5) | async-done | bytes 1966112 | tf_op jit(solution)/shard_map/all_to_all | solution.py:272
  (92 shorter events, 58.2 us)
Async XLA Ops:
  8.0 56.6 %all-gather.6.cloned.1.call-start = ((), (), s32[]{:S(2)}) async-start(), calls=%async_computation.7 | async-start | bytes 2621440 | tf_op jit(solution)/shard_map/all_gather | solution.py:192
  21.1 22.3 %copy-start.9 = (bf16[3,128,2048]{2,1,0:T(8,128)(2,1)S(1)}, bf16[3,128,2048]{2,1,0:T(8,128)(2,1)}, u32[]{:S(2)}) copy-start(bf16[3,128,2048]{2,1,0:T(8,128)(2,1)} %param.8) | copy-start | bytes 4718596
  46.0 51.4 %all-to-all-start = ((bf16[3,128,2048]{1,0,2:T(4,128)(2,1)}), bf16[3,128,2048]{1,0,2:T(4,128)(2,1)S(1)}, u32[]{:S(2)}, u32[]{:S(2)}) async-start(bf16[3,128,2048]{1,0,2:T(4,128)(2,1)} %copy.66), calls=%async_computation | async-start | bytes 4194304 | tf_op jit(solution)/shard_map/all_to_all | solution.py:187
  67.3 5.4 %copy-start.2 = (bf16[8,128,1024]{2,1,0:T(8,128)(2,1)}, bf16[8,128,1024]{2,1,0:T(8,128)(2,1)S(1)}, u32[]{:S(2)}) copy-start(bf16[8,128,1024]{2,1,0:T(8,128)(2,1)S(1)} %copy.78) | copy-start | bytes 6291460
  67.3 3.1 %copy-start.7 = (bf16[1024,4,1,256]{0,3,2,1:T(8,128)(2,1)S(1)}, bf16[1024,4,1,256]{0,3,2,1:T(8,128)(2,1)}, u32[]{:S(2)}) copy-start(bf16[1024,4,1,256]{0,3,2,1:T(8,128)(2,1)} %get-tuple-element.46) | copy-start | bytes 6291460
  68.5 4.2 %copy-start.11 = (bf16[4,128,1024]{2,1,0:T(8,128)(2,1)}, bf16[4,128,1024]{2,1,0:T(8,128)(2,1)S(1)}, u32[]{:S(2)}) copy-start(bf16[4,128,1024]{2,1,0:T(8,128)(2,1)S(1)} %get-tuple-element.50) | copy-start | bytes 3145732
  72.7 35.0 %collective-permute-start = (bf16[512,1024]{0,1:T(8,128)(2,1)}, bf16[512,1024]{0,1:T(8,128)(2,1)}, u32[]{:S(2)}, u32[]{:S(2)}) collective-permute-start(bf16[512,1024]{0,1:T(8,128)(2,1)} %fusion.7), channel_id=1, source_target_pairs={{0,4},{4,0},{8,12},{12,8},{16,20},{20,16},{24,28},{28,24},{1,5},{5... | collective-permute-start | bytes 3145736 | tf_op jit(solution)/shard_map/ppermute | solution.py:229
  101.4 2.6 copy-start.8
  101.4 2.6 copy-start.10
  104.0 3.7 %copy-start.6 = (bf16[1024,4,1,256]{0,3,2,1:T(8,128)(2,1)S(1)}, bf16[1024,4,1,256]{0,3,2,1:T(8,128)(2,1)}, u32[]{:S(2)}) copy-start(bf16[1024,4,1,256]{0,3,2,1:T(8,128)(2,1)} %get-tuple-element.45) | copy-start | bytes 6291460
  104.0 3.7 %copy-start.12 = (bf16[4,128,1024]{2,1,0:T(8,128)(2,1)S(1)}, bf16[4,128,1024]{2,1,0:T(8,128)(2,1)}, u32[]{:S(2)}) copy-start(bf16[4,128,1024]{2,1,0:T(8,128)(2,1)} %copy-done.11) | copy-start | bytes 3145732
  106.3 26.4 %collective-permute-start.1 = (bf16[512,1024]{0,1:T(8,128)(2,1)}, bf16[512,1024]{0,1:T(8,128)(2,1)}, u32[]{:S(2)}, u32[]{:S(2)}) collective-permute-start(bf16[512,1024]{0,1:T(8,128)(2,1)} %fusion.8), channel_id=1, source_target_pairs={{0,4},{4,0},{8,12},{12,8},{16,20},{20,16},{24,28},{28,24},{1,5},{5... | collective-permute-start | bytes 3145736 | tf_op jit(solution)/shard_map/ppermute | solution.py:229
  111.3 29.3 %all-to-all-start.3 = ((bf16[1,512,4,256]{1,3,0,2:T(8,128)(2,1)}), bf16[1,512,4,256]{1,3,0,2:T(8,128)(2,1)}, u32[]{:S(2)}, u32[]{:S(2)}) async-start(bf16[1,512,4,256]{1,3,0,2:T(8,128)(2,1)} %bitcast.21), calls=%async_computation.3 | async-start | bytes 2097152 | tf_op jit(solution)/shard_map/all_to_all | solution.py:232
  115.6 108.2 %all-gather.4.cloned.1.call-start = ((), (), s32[]{:S(2)}) async-start(), calls=%async_computation.6 | async-start | bytes 4718592 | tf_op jit(solution)/shard_map/all_gather | solution.py:214
  121.6 1.7 copy-start.1
  140.6 43.3 %all-to-all-start.4 = ((bf16[1,512,4,256]{1,3,0,2:T(8,128)(2,1)}), bf16[1,512,4,256]{1,3,0,2:T(8,128)(2,1)}, u32[]{:S(2)}, u32[]{:S(2)}) async-start(bf16[1,512,4,256]{1,3,0,2:T(8,128)(2,1)} %bitcast.126), calls=%async_computation.4 | async-start | bytes 2097152 | tf_op jit(solution)/shard_map/all_to_all | solution.py:232
  148.9 40.3 %copy-start.5 = (f32[1,1024,256]{2,1,0:T(8,128)S(1)}, f32[1,1024,256]{2,1,0:T(8,128)}, u32[]{:S(2)}) copy-start(f32[1,1024,256]{2,1,0:T(8,128)} %copy.89) | copy-start | bytes 3145732
  191.6 11.8 %copy-start.4 = (f32[1,1024,256]{1,2,0:T(8,128)S(1)}, f32[1,1024,256]{1,2,0:T(8,128)}, u32[]{:S(2)}) copy-start(f32[1,1024,256]{1,2,0:T(8,128)} %copy.87) | copy-start | bytes 3145732
  203.6 2.7 copy-start
  215.0 8.9 %copy-start.3 = (bf16[8,128,1024]{2,1,0:T(8,128)(2,1)S(1)}, bf16[8,128,1024]{2,1,0:T(8,128)(2,1)}, u32[]{:S(2)}) copy-start(bf16[8,128,1024]{2,1,0:T(8,128)(2,1)} %copy-done.2) | copy-start | bytes 6291460
  218.0 49.9 %all-to-all-start.5 = ((bf16[8,480,256]{2,1,0:T(8,128)(2,1)}), bf16[8,480,256]{2,1,0:T(8,128)(2,1)}, u32[]{:S(2)}, u32[]{:S(2)}) async-start(bf16[8,480,256]{2,1,0:T(8,128)(2,1)} %pad_maximum_fusion.1), calls=%async_computation.5 | async-start | bytes 3932160 | tf_op jit(solution)/shard_map/all_to_all | solution.py:272
Sparse Core Ops, SparseCore 0:
  43.6 20.9 all-gather.5
Sparse Core Ops, SparseCore 1:
  132.8 91.0 all-gather.3

commit v3 on v2

--- a/solution.py
+++ b/solution.py
@@ -177,6 +177,19 @@
     return jnp.swapaxes(series, 0, 1).reshape(CHUNKS * steps, width)
 
 
+def exchange(blocks, axis):
+    devices, index = lax.axis_size(axis), lax.axis_index(axis)
+    came = []
+    for shift in range(devices):
+        target = lax.rem(index + shift, devices)
+        block = lax.dynamic_index_in_dim(blocks, target, axis=0, keepdims=False)
+        if shift:
+            block = lax.ppermute(block, axis, [(i, (i + shift) % devices) for i in range(devices)])
+        came.append(block)
+    turned = jnp.stack(came[::-1] + came[::-1])
+    return lax.dynamic_slice_in_dim(turned, devices - 1 - index, devices, axis=0)
+
+
 def on_device(out_grad, out_weight, projections, short_filters, residues, decay_rates):
     devices, index = lax.axis_size("ctx"), lax.axis_index("ctx")
     panels = lax.axis_size("fsdp")
@@ -187,9 +200,11 @@
     series = lax.all_to_all(projections, "ctx", split_axis=2, concat_axis=1, tiled=True)
 
     rows = tokens // panels
-    mine = lax.all_to_all(out_grad, "fsdp", split_axis=0, concat_axis=1, tiled=True)
-    mine = lax.all_to_all(mine, "ctx", split_axis=1, concat_axis=0, tiled=True)
-    mine = lax.all_gather(mine.reshape(devices, rows, -1), "fsdp", axis=1)
+    mine = exchange(out_grad.reshape(panels, rows, wide), "fsdp")
+    mine = mine.reshape(panels, rows, -1, wide * panels // devices)
+    mine = jnp.transpose(mine, (0, 2, 1, 3)).reshape(devices, rows, -1)
+    mine = exchange(mine, "ctx")
+    mine = lax.all_gather(mine, "fsdp", axis=1)
     cotangent = mine.reshape(length, -1)
 
     def own(array):

time: 283 us -> 298 us (1.053)
  blocking collectives: 33.5 us -> 73.5 us
  other arithmetic: 30.2 us -> 12.8 us
  local copies, waits for them, and re-layouts: 53.8 us -> 40.9 us
  starting transfers between devices: 19.9 us -> 30.5 us
  waiting for transfers between devices: 94.2 us -> 91.1 us
    ppermute x2, waiting for transfers between devices: 0.01 us -> 48.7 us  [on_device(): other = lax.ppermute(sent.astype(jnp.bfloat16), 'ctx', swap)]
    all_to_all x2 -> x1, blocking collectives: 33.5 us -> 73.5 us  [on_device(): got = lax.all_to_all(sent, 'ctx', 0, 0)]
    all_to_all x1 -> x0, waiting for transfers between devices: 29.3 us -> none  [on_device(): got = lax.all_to_all(sent, 'ctx', 0, 0)]
    all_to_all x1, waiting for transfers between devices: 22.4 us -> 0.01 us  [on_device(): lax.all_to_all(projections, 'ctx', split_axis=2, concat_axis=1, tiled=True)]
    ppermute x0 -> x10, starting transfers between devices: none -> 14.5 us  [exchange(): lax.ppermute(block, axis, [(i, (i + shift) % devices) for i in range(devi...]
    ppermute x0 -> x10, waiting for transfers between devices: none -> 13.6 us  [exchange(): lax.ppermute(block, axis, [(i, (i + shift) % devices) for i in range(devi...]
    all_to_all x2, waiting for transfers between devices: 38.4 us -> 26 us  [on_device(): lax.all_to_all(both.reshape(-1, outer, share), 'ctx', 1, 0, axis_index_gr...]
    another operation x0 -> x6, local copies, waits for them, and re-layouts: none -> 8.86 us  [the longest x4 7.93 us: on_device(): lax.all_to_all(both.reshape(-1, outer, share), 'ctx', 1, 0, axis_index_gr...]
  transfers between devices with their start and end apart: 8 -> 17, of which waited for: 6 -> 8; matrix products, arithmetic and copies ran while one was open for 33% -> 20% of each run, Pallas kernels for 5% -> 4%
where the time goes in v3:
time: 298 us; the launch traced here: 297 us
  waiting for transfers between devices  91.1 us (31%)
  blocking collectives  73.5 us (25%)
  local copies, waits for them, and re-layouts  40.9 us (14%)
  starting transfers between devices  30.5 us (10%)
  matrix products  19.6 us (7%)
  between operations  16.1 us (5%)
  Pallas kernels  13 us (4%)
  other arithmetic  12.8 us (4%)
    all_to_all x1, blocking collectives, on_device(): got = lax.all_to_all(sent, 'ctx', 0, 0)  73.5 us
    ppermute x2, waiting for transfers between devices, on_device(): other = lax.ppermute(sent.astype(jnp.bfloat16), 'ctx', swap)  48.7 us
    all_to_all x2, waiting for transfers between devices, on_device(): lax.all_to_all(both.reshape(-1, outer, share), 'ctx', 1, 0, axis_index_gr...  26 us
    ppermute x10, starting transfers between devices, exchange(): lax.ppermute(block, axis, [(i, (i + shift) % devices) for i in range(devi...  14.5 us
    ppermute x10, waiting for transfers between devices, exchange(): lax.ppermute(block, axis, [(i, (i + shift) % devices) for i in range(devi...  13.6 us
    unnamed x51, local copies, waits for them, and re-layouts  12.6 us
    all_to_all x2, starting transfers between devices, on_device(): lax.all_to_all(both.reshape(-1, outer, share), 'ctx', 1, 0, axis_index_gr...  10.9 us
    pallas_call x1, Pallas kernels, run_backward(): pl.pallas_call(backward_kernel, grid=(width // lanes,), in_specs=[series,...  8.96 us
  transfers between devices with their start and end apart: 17, of which 8 were waited for; matrix products, arithmetic and copies ran while one was open for 20% of the time, Pallas kernels for 4%

profile of v3, /device:TPU:0, one launch (start us, length us, event | category | flops | bytes accessed | tf_op | source)
XLA Modules:
  0.0 297.4 jit_solution(14113342058659698541)
XLA Ops:
  12.4 3.0 collective-permute-done
  15.4 3.8 %collective-permute-done.1 = bf16[32,2048]{1,0:T(8,128)(2,1)S(1)} collective-permute-done((bf16[32,2048]{1,0:T(8,128)(2,1)S(1)}, bf16[32,2048]{1,0:T(8,128)(2,1)S(1)}, u32[]{:S(2)}, u32[]{:S(2)}) %collective-permute-start.1) | collective-permute-done | bytes 131104 | tf_op jit(solution)/shard_map/ppermute | solution.py:187
  21.2 4.7 %collective-permute-start.3 = (bf16[32,1024]{1,0:T(8,128)(2,1)S(1)}, bf16[32,1024]{1,0:T(8,128)(2,1)S(1)}, u32[]{:S(2)}, u32[]{:S(2)}) collective-permute-start(bf16[32,1024]{1,0:T(8,128)(2,1)S(1)} %get-tuple-element.35), channel_id=1, source_target_pairs={{0,28},{4,0},{8,4},{12,8},{16,12},{20,16},{24,20},{28,24},{1,29},{... | collective-permute-start | bytes 196616 | tf_op jit(solution)/shard_map/ppermute | solution.py:187
  26.4 3.0 %collective-permute-start.6 = (bf16[32,1024]{1,0:T(8,128)(2,1)S(1)}, bf16[32,1024]{1,0:T(8,128)(2,1)S(1)}, u32[]{:S(2)}, u32[]{:S(2)}) collective-permute-start(bf16[32,1024]{1,0:T(8,128)(2,1)S(1)} %get-tuple-element.32), channel_id=1, source_target_pairs={{0,16},{4,20},{8,24},{12,28},{16,0},{20,4},{24,8},{28,12},{1,17},{... | collective-permute-start | bytes 196616 | tf_op jit(solution)/shard_map/ppermute | solution.py:187
  32.5 2.9 collective-permute-done.6
  35.4 4.0 %collective-permute-done.7 = bf16[32,1024]{1,0:T(8,128)(2,1)S(1)} collective-permute-done((bf16[32,1024]{1,0:T(8,128)(2,1)S(1)}, bf16[32,1024]{1,0:T(8,128)(2,1)S(1)}, u32[]{:S(2)}, u32[]{:S(2)}) %collective-permute-start.7) | collective-permute-done | bytes 65568 | tf_op jit(solution)/shard_map/ppermute | solution.py:187
  43.0 3.6 %all-to-all-start = ((bf16[3,128,2048]{1,0,2:T(4,128)(2,1)}), bf16[3,128,2048]{1,0,2:T(4,128)(2,1)S(1)}, u32[]{:S(2)}, u32[]{:S(2)}) async-start(bf16[3,128,2048]{1,0,2:T(4,128)(2,1)} %copy.50), calls=%async_computation | async-start | bytes 4194304 | tf_op jit(solution)/shard_map/all_to_all | solution.py:200
  46.6 6.4 %copy.56 = bf16[1024,2048]{0,1:T(8,128)(2,1)} copy(bf16[1024,2048]{1,0:T(8,128)(2,1)} %param.7) | data formatting | bytes 8388608 | tf_op args[1]
  53.0 4.7 %constant_dynamic-slice_fusion.3 = (bf16[1024,4,1,256]{0,3,2,1:T(8,128)(2,1)}, bf16[1024,4,1,256]{0,3,2,1:T(8,128)(2,1)}) fusion(bf16[1024,4,2,256]{0,3,2,1:T(8,128)(2,1)} %bitcast.133, s32[]{:T(128)S(6)} %select_n.72, s32[]{:T(128)S(6)} %select_n.71), kind=kLoop, calls=%fused_computation.79 | loop fusion | bytes 8388616 | tf_op jit(solution)/shard_map/jit(dynamic_index_in_dim)/dynamic_slice | solution.py:235
  57.7 2.8 all-gather.6.cloned.1.call-done
  60.5 2.8 fusion.4
  66.2 31.4 %collective-permute-done.10 = bf16[512,1024]{1,0:T(8,128)(2,1)S(1)} collective-permute-done((bf16[512,1024]{1,0:T(8,128)(2,1)S(1)}, bf16[512,1024]{1,0:T(8,128)(2,1)S(1)}, u32[]{:S(2)}, u32[]{:S(2)}) %collective-permute-start.10) | collective-permute-done | bytes 1048608 | tf_op jit(solution)/shard_map/ppermute | solution.py:244
  102.8 6.1 %all-to-all-start.1 = ((bf16[1,512,4,256]{3,1,0,2:T(8,128)(2,1)}), bf16[1,512,4,256]{3,1,0,2:T(8,128)(2,1)}, u32[]{:S(2)}, u32[]{:S(2)}) async-start(bf16[1,512,4,256]{3,1,0,2:T(8,128)(2,1)} %copy.57), calls=%async_computation.1 | async-start | bytes 2097152 | tf_op jit(solution)/shard_map/all_to_all | solution.py:247
  108.9 4.2 %convolution_convert_fusion.1 = bf16[512,1024]{1,0:T(8,128)(2,1)} fusion(bf16[512,1024]{1,0:T(8,128)(2,1)} %bitcast.155, bf16[1024,1024]{0,1:T(8,128)(2,1)} %bitcast.151), kind=kOutput, calls=%fused_computation.13 | convolution fusion | flops 1074266112 | bytes 4194304 | tf_op jit(solution)/shard_map/dot_general | solution.py:243
  116.3 2.6 copy.52
  120.8 17.3 %collective-permute-done.11 = bf16[512,1024]{1,0:T(8,128)(2,1)} collective-permute-done((bf16[512,1024]{1,0:T(8,128)(2,1)}, bf16[512,1024]{1,0:T(8,128)(2,1)}, u32[]{:S(2)}, u32[]{:S(2)}) %collective-permute-start.11) | collective-permute-done | bytes 1048608 | tf_op jit(solution)/shard_map/ppermute | solution.py:244
  138.0 3.5 %add_convert_fusion.1 = bf16[512,1024]{1,0:T(8,128)(2,1)} fusion(bf16[512,1024]{1,0:T(8,128)(2,1)} %collective-permute-done.11, bf16[512,1024]{1,0:T(8,128)(2,1)S(1)} %bitcast.156, bf16[1024,1024]{0,1:T(8,128)(2,1)S(1)} %bitcast.150), kind=kOutput, calls=%fused_computation.8 | convolution fusion | flops 1075314688 | bytes 5242880 | tf_op jit(solution)/shard_map/dot_general | solution.py:245
  141.5 2.6 broadcast_in_dim_reshape.7
  146.5 4.8 %all-to-all-start.2 = ((bf16[1,512,4,256]{3,1,0,2:T(8,128)(2,1)}), bf16[1,512,4,256]{3,1,0,2:T(8,128)(2,1)}, u32[]{:S(2)}, u32[]{:S(2)}) async-start(bf16[1,512,4,256]{3,1,0,2:T(8,128)(2,1)} %copy.58), calls=%async_computation.2 | async-start | bytes 2097152 | tf_op jit(solution)/shard_map/all_to_all | solution.py:247
  154.2 4.0 %shard_map.101 = (f32[128,8,256]{2,1,0:T(8,128)S(1)}, f32[16,8,256]{2,1,0:T(8,128)S(1)}) custom-call(f32[128,8,256]{2,1,0:T(8,128)S(1)} %bitcast.129, f32[16,1,256]{2,1,0:T(1,128)S(1)} %copy.54.decay_ref, f32[16,1,256]{2,1,0:T(1,128)S(1)} %broadcast_in_dim.16.jump_ref, f32[16,1,256]{2,1,0:T(1,128)S(1)} %broadcast_in_dim.17.res_ref), custom_call_target="tpu_custom_call" | custom-call | flops 25165824 | bytes 2097152 | tf_op jit(solution)/shard_map/pallas_call | solution.py:125
  161.1 26.0 %all-to-all-done.2 = bf16[1,512,4,256]{3,1,0,2:T(8,128)(2,1)} async-done(((bf16[1,512,4,256]{3,1,0,2:T(8,128)(2,1)}), bf16[1,512,4,256]{3,1,0,2:T(8,128)(2,1)}, u32[]{:S(2)}, u32[]{:S(2)}) %all-to-all-start.2) | async-done | bytes 1048608 | tf_op jit(solution)/shard_map/all_to_all | solution.py:247
  189.8 9.0 %shard_map.102 = (f32[128,8,256]{2,1,0:T(8,128)S(1)}, f32[16,1,256]{2,1,0:T(1,128)S(1)}, f32[16,1,256]{2,1,0:T(1,128)S(1)}) custom-call(f32[128,8,256]{2,1,0:T(8,128)S(1)} %bitcast.130, f32[128,8,256]{2,1,0:T(8,128)S(1)} %fusion.1.gl_ref, f32[16,1,256]{2,1,0:T(1,128)S(1)} %copy.54.decay_ref, f32[16,1,256]{2,1,0:T(1,128)S(1)} %broadcast_in_dim.16.jump_ref, ...), custom_call_target="tpu_custom_call" | custom-call | flops 50331648 | bytes 3145728 | tf_op jit(solution)/shard_map/pallas_call | solution.py:148
  204.6 73.5 %all_to_all.41 = bf16[8,480,256]{2,1,0:T(8,128)(2,1)S(1)} all-to-all(bf16[8,480,256]{2,1,0:T(8,128)(2,1)S(1)} %pad_maximum_fusion.1), channel_id=1, replica_groups=mesh['ctx'=8,'fsdp'=4] {'ctx'}, dimensions={0} | all-to-all | bytes 3932160 | tf_op jit(solution)/shard_map/all_to_all | solution.py:287
  281.6 8.3 %convolution_convert_fusion = bf16[1024,2048]{1,0:T(8,128)(2,1)} fusion(bf16[1024,1024]{1,0:T(8,128)(2,1)S(1)} %bitcast.153, bf16[1024,2048]{1,0:T(8,128)(2,1)} %all-gather.4.cloned.1.call-done), kind=kOutput, calls=%fused_computation | convolution fusion | flops 4297064448 | bytes 10485760 | tf_op jit(solution)/shard_map/dot_general | solution.py:253
  (124 shorter events, 46.4 us)
Async XLA Ops:
  8.0 52.5 %all-gather.6.cloned.1.call-start = ((), (), s32[]{:S(2)}) async-start(), calls=%async_computation.5 | async-start | bytes 2621440 | tf_op jit(solution)/shard_map/all_gather | solution.py:207
  9.1 6.2 %collective-permute-start = (bf16[32,2048]{1,0:T(8,128)(2,1)S(1)}, bf16[32,2048]{1,0:T(8,128)(2,1)S(1)}, u32[]{:S(2)}, u32[]{:S(2)}) collective-permute-start(bf16[32,2048]{1,0:T(8,128)(2,1)S(1)} %get-tuple-element.38), channel_id=1, source_target_pairs={{0,3},{1,0},{2,1},{3,2},{4,7},{5,4},{6,5},{7,6},{8,11},{9,8},{10,9... | collective-permute-start | bytes 393224 | tf_op jit(solution)/shard_map/ppermute | solution.py:187
  11.6 7.5 %collective-permute-start.1 = (bf16[32,2048]{1,0:T(8,128)(2,1)S(1)}, bf16[32,2048]{1,0:T(8,128)(2,1)S(1)}, u32[]{:S(2)}, u32[]{:S(2)}) collective-permute-start(bf16[32,2048]{1,0:T(8,128)(2,1)S(1)} %get-tuple-element.37), channel_id=1, source_target_pairs={{0,2},{1,3},{2,0},{3,1},{4,6},{5,7},{6,4},{7,5},{8,10},{9,11},{10,... | collective-permute-start | bytes 393224 | tf_op jit(solution)/shard_map/ppermute | solution.py:187
  12.2 6.9 %collective-permute-start.2 = (bf16[32,2048]{1,0:T(8,128)(2,1)S(1)}, bf16[32,2048]{1,0:T(8,128)(2,1)S(1)}, u32[]{:S(2)}, u32[]{:S(2)}) collective-permute-start(bf16[32,2048]{1,0:T(8,128)(2,1)S(1)} %get-tuple-element.36), channel_id=1, source_target_pairs={{0,1},{1,2},{2,3},{3,0},{4,5},{5,6},{6,7},{7,4},{8,9},{9,10},{10,1... | collective-permute-start | bytes 393224 | tf_op jit(solution)/shard_map/ppermute | solution.py:187
  21.1 19.4 %copy-start.9 = (bf16[3,128,2048]{2,1,0:T(8,128)(2,1)S(1)}, bf16[3,128,2048]{2,1,0:T(8,128)(2,1)}, u32[]{:S(2)}) copy-start(bf16[3,128,2048]{2,1,0:T(8,128)(2,1)} %param.8) | copy-start | bytes 4718596
  21.2 8.2 %collective-permute-start.3 = (bf16[32,1024]{1,0:T(8,128)(2,1)S(1)}, bf16[32,1024]{1,0:T(8,128)(2,1)S(1)}, u32[]{:S(2)}, u32[]{:S(2)}) collective-permute-start(bf16[32,1024]{1,0:T(8,128)(2,1)S(1)} %get-tuple-element.35), channel_id=1, source_target_pairs={{0,28},{4,0},{8,4},{12,8},{16,12},{20,16},{24,20},{28,24},{1,29},{... | collective-permute-start | bytes 196616 | tf_op jit(solution)/shard_map/ppermute | solution.py:187
  26.0 5.3 %collective-permute-start.4 = (bf16[32,1024]{1,0:T(8,128)(2,1)S(1)}, bf16[32,1024]{1,0:T(8,128)(2,1)S(1)}, u32[]{:S(2)}, u32[]{:S(2)}) collective-permute-start(bf16[32,1024]{1,0:T(8,128)(2,1)S(1)} %get-tuple-element.34), channel_id=1, source_target_pairs={{0,24},{4,28},{8,0},{12,4},{16,8},{20,12},{24,16},{28,20},{1,25},{... | collective-permute-start | bytes 196616 | tf_op jit(solution)/shard_map/ppermute | solution.py:187
  26.4 6.0 %collective-permute-start.5 = (bf16[32,1024]{1,0:T(8,128)(2,1)S(1)}, bf16[32,1024]{1,0:T(8,128)(2,1)S(1)}, u32[]{:S(2)}, u32[]{:S(2)}) collective-permute-start(bf16[32,1024]{1,0:T(8,128)(2,1)S(1)} %get-tuple-element.33), channel_id=1, source_target_pairs={{0,20},{4,24},{8,28},{12,0},{16,4},{20,8},{24,12},{28,16},{1,21},{... | collective-permute-start | bytes 196616 | tf_op jit(solution)/shard_map/ppermute | solution.py:187
  26.4 8.9 %collective-permute-start.6 = (bf16[32,1024]{1,0:T(8,128)(2,1)S(1)}, bf16[32,1024]{1,0:T(8,128)(2,1)S(1)}, u32[]{:S(2)}, u32[]{:S(2)}) collective-permute-start(bf16[32,1024]{1,0:T(8,128)(2,1)S(1)} %get-tuple-element.32), channel_id=1, source_target_pairs={{0,16},{4,20},{8,24},{12,28},{16,0},{20,4},{24,8},{28,12},{1,17},{... | collective-permute-start | bytes 196616 | tf_op jit(solution)/shard_map/ppermute | solution.py:187
  29.4 9.9 %collective-permute-start.7 = (bf16[32,1024]{1,0:T(8,128)(2,1)S(1)}, bf16[32,1024]{1,0:T(8,128)(2,1)S(1)}, u32[]{:S(2)}, u32[]{:S(2)}) collective-permute-start(bf16[32,1024]{1,0:T(8,128)(2,1)S(1)} %get-tuple-element.31), channel_id=1, source_target_pairs={{0,12},{4,16},{8,20},{12,24},{16,28},{20,0},{24,4},{28,8},{1,13},{... | collective-permute-start | bytes 196616 | tf_op jit(solution)/shard_map/ppermute | solution.py:187
  29.4 9.9 %collective-permute-start.8 = (bf16[32,1024]{1,0:T(8,128)(2,1)S(1)}, bf16[32,1024]{1,0:T(8,128)(2,1)S(1)}, u32[]{:S(2)}, u32[]{:S(2)}) collective-permute-start(bf16[32,1024]{1,0:T(8,128)(2,1)S(1)} %get-tuple-element.30), channel_id=1, source_target_pairs={{0,8},{4,12},{8,16},{12,20},{16,24},{20,28},{24,0},{28,4},{1,9},{5... | collective-permute-start | bytes 196616 | tf_op jit(solution)/shard_map/ppermute | solution.py:187
  31.3 8.1 %collective-permute-start.9 = (bf16[32,1024]{1,0:T(8,128)(2,1)S(1)}, bf16[32,1024]{1,0:T(8,128)(2,1)S(1)}, u32[]{:S(2)}, u32[]{:S(2)}) collective-permute-start(bf16[32,1024]{1,0:T(8,128)(2,1)S(1)} %get-tuple-element.29), channel_id=1, source_target_pairs={{0,4},{4,8},{8,12},{12,16},{16,20},{20,24},{24,28},{28,0},{1,5},{5... | collective-permute-start | bytes 196616 | tf_op jit(solution)/shard_map/ppermute | solution.py:187
  43.0 59.8 %all-to-all-start = ((bf16[3,128,2048]{1,0,2:T(4,128)(2,1)}), bf16[3,128,2048]{1,0,2:T(4,128)(2,1)S(1)}, u32[]{:S(2)}, u32[]{:S(2)}) async-start(bf16[3,128,2048]{1,0,2:T(4,128)(2,1)} %copy.50), calls=%async_computation | async-start | bytes 4194304 | tf_op jit(solution)/shard_map/all_to_all | solution.py:200
  63.4 34.3 %copy-start.5 = (bf16[1024,4,1,256]{0,3,2,1:T(8,128)(2,1)S(1)}, bf16[1024,4,1,256]{0,3,2,1:T(8,128)(2,1)}, u32[]{:S(2)}) copy-start(bf16[1024,4,1,256]{0,3,2,1:T(8,128)(2,1)} %get-tuple-element.21) | copy-start | bytes 6291460
  64.7 32.9 %collective-permute-start.10 = (bf16[512,1024]{1,0:T(8,128)(2,1)S(1)}, bf16[512,1024]{1,0:T(8,128)(2,1)S(1)}, u32[]{:S(2)}, u32[]{:S(2)}) collective-permute-start(bf16[512,1024]{1,0:T(8,128)(2,1)S(1)} %convolution_convert_fusion.2), channel_id=1, source_target_pairs={{0,4},{4,0},{8,12},{12,8},{16,20},{20,16},{24,28},{28,24},{1,5},{5... | collective-permute-start | bytes 3145736 | tf_op jit(solution)/shard_map/ppermute | solution.py:244
  102.8 43.7 %all-to-all-start.1 = ((bf16[1,512,4,256]{3,1,0,2:T(8,128)(2,1)}), bf16[1,512,4,256]{3,1,0,2:T(8,128)(2,1)}, u32[]{:S(2)}, u32[]{:S(2)}) async-start(bf16[1,512,4,256]{3,1,0,2:T(8,128)(2,1)} %copy.57), calls=%async_computation.1 | async-start | bytes 2097152 | tf_op jit(solution)/shard_map/all_to_all | solution.py:247
  113.1 24.9 %collective-permute-start.11 = (bf16[512,1024]{1,0:T(8,128)(2,1)}, bf16[512,1024]{1,0:T(8,128)(2,1)}, u32[]{:S(2)}, u32[]{:S(2)}) collective-permute-start(bf16[512,1024]{1,0:T(8,128)(2,1)} %convolution_convert_fusion.1), channel_id=1, source_target_pairs={{0,4},{4,0},{8,12},{12,8},{16,20},{20,16},{24,28},{28,24},{1,5},{5... | collective-permute-start | bytes 3145736 | tf_op jit(solution)/shard_map/ppermute | solution.py:244
  118.9 19.2 %copy-start.6 = (bf16[1024,4,1,256]{0,3,2,1:T(8,128)(2,1)S(1)}, bf16[1024,4,1,256]{0,3,2,1:T(8,128)(2,1)}, u32[]{:S(2)}) copy-start(bf16[1024,4,1,256]{0,3,2,1:T(8,128)(2,1)} %get-tuple-element.21) | copy-start | bytes 6291460
  118.9 19.2 %copy-start.10 = (bf16[4,128,1024]{2,1,0:T(8,128)(2,1)S(1)}, bf16[4,128,1024]{2,1,0:T(8,128)(2,1)}, u32[]{:S(2)}) copy-start(bf16[4,128,1024]{2,1,0:T(8,128)(2,1)} %get-tuple-element.26) | copy-start | bytes 3145732
  120.8 30.6 %copy-start = (f32[3,1026,256]{2,1,0:T(8,128)}, f32[3,1026,256]{2,1,0:T(8,128)S(1)}, u32[]{:S(2)}) copy-start(f32[3,1026,256]{2,1,0:T(8,128)S(1)} %pad_convert_fusion) | copy-start | bytes 9455620
  146.5 40.6 %all-to-all-start.2 = ((bf16[1,512,4,256]{3,1,0,2:T(8,128)(2,1)}), bf16[1,512,4,256]{3,1,0,2:T(8,128)(2,1)}, u32[]{:S(2)}, u32[]{:S(2)}) async-start(bf16[1,512,4,256]{3,1,0,2:T(8,128)(2,1)} %copy.58), calls=%async_computation.2 | async-start | bytes 2097152 | tf_op jit(solution)/shard_map/all_to_all | solution.py:247
  151.3 130.3 %all-gather.4.cloned.1.call-start = ((), (), s32[]{:S(2)}) async-start(), calls=%async_computation.4 | async-start | bytes 4718592 | tf_op jit(solution)/shard_map/all_gather | solution.py:229
  152.3 6.3 %copy-start.2 = (f32[3,1024,256]{2,1,0:T(8,128)}, f32[3,1024,256]{2,1,0:T(8,128)S(1)}, u32[]{:S(2)}) copy-start(f32[3,1024,256]{2,1,0:T(8,128)S(1)} %multiply_add_fusion) | copy-start | bytes 9437188
  278.1 3.5 %copy-start.8 = (bf16[8,128,1024]{2,1,0:T(8,128)(2,1)S(1)}, bf16[8,128,1024]{2,1,0:T(8,128)(2,1)}, u32[]{:S(2)}) copy-start(bf16[8,128,1024]{2,1,0:T(8,128)(2,1)} %all-gather.6.cloned.1.call-done) | copy-start | bytes 6291460
  (4 other events, 9.1 us)
Sparse Core Ops, SparseCore 0:
  40.6 19.9 all-gather.5
Sparse Core Ops, SparseCore 1:
  159.8 110.3 all-gather.3

commit v4 on v3

--- a/solution.py
+++ b/solution.py
@@ -205,7 +205,7 @@
     mine = jnp.transpose(mine, (0, 2, 1, 3)).reshape(devices, rows, -1)
     mine = exchange(mine, "ctx")
     mine = lax.all_gather(mine, "fsdp", axis=1)
-    cotangent = mine.reshape(length, -1)
+    cotangent, series = lax.optimization_barrier((mine.reshape(length, -1), series))
 
     def own(array):
         return lax.dynamic_slice_in_dim(array, index * share, share, axis=array.ndim - 1)
@@ -226,8 +226,6 @@
     long_chunks, entry = run_forward(kv, decay, jump, res)
     long_out = from_chunks(long_chunks)
     y_rounded = (q_branch * long_out).astype(jnp.bfloat16)
-    y_all = lax.all_gather(y_rounded, "ctx", axis=1, tiled=True)
-
     outer, side = devices // 2, lax.rem(index, 2)
     paired = out_weight.reshape(out_weight.shape[0], outer, 2, share)
 
@@ -244,9 +242,12 @@
         other = lax.ppermute(sent.astype(jnp.bfloat16), "ctx", swap)
         kept = jnp.dot(piece, ours, preferred_element_type=jnp.float32)
         both = (kept + other.astype(jnp.float32)).astype(jnp.bfloat16)
+        both, y_rounded = lax.optimization_barrier((both, y_rounded))
         terms = lax.all_to_all(
             both.reshape(-1, outer, share), "ctx", 1, 0, axis_index_groups=lanes_of
         )
+        if not pieces:
+            y_all = lax.all_gather(y_rounded, "ctx", axis=1, tiled=True)
         pieces.append(jnp.sum(terms.astype(jnp.float32), axis=0))
     grad_y = jnp.concatenate(pieces, axis=0)
 

time: 298 us -> 338 us (1.13)
  waiting for transfers between devices: 91.1 us -> 140 us
  blocking collectives: 73.5 us -> 69.5 us
    all_to_all x1, waiting for transfers between devices: 0.01 us -> 33.8 us  [on_device(): lax.all_to_all(projections, 'ctx', split_axis=2, concat_axis=1, tiled=True)]
    all_to_all x2, waiting for transfers between devices: 26 us -> 56.8 us  [on_device(): lax.all_to_all(both.reshape(-1, outer, share), 'ctx', 1, 0, axis_index_gr...]
    ppermute x2, waiting for transfers between devices: 48.7 us -> 34.9 us  [on_device(): other = lax.ppermute(sent.astype(jnp.bfloat16), 'ctx', swap)]
    all_to_all x1, blocking collectives: 73.5 us -> 69.5 us  [on_device(): got = lax.all_to_all(sent, 'ctx', 0, 0)]
    unnamed x51 -> x53, local copies, waits for them, and re-layouts: 12.6 us -> 14.3 us
  transfers between devices with their start and end apart: 17 -> 17, of which waited for: 8 -> 8; matrix products, arithmetic and copies ran while one was open for 20% -> 13% of each run, Pallas kernels for 4% -> 4%
where the time goes in v4:
time: 338 us; the launch traced here: 337 us
  waiting for transfers between devices  140 us (41%)
  blocking collectives  69.5 us (21%)
  local copies, waits for them, and re-layouts  39 us (12%)
  starting transfers between devices  28.1 us (8%)
  matrix products  22 us (7%)
  between operations  14.7 us (4%)
  Pallas kernels  13 us (4%)
  other arithmetic  11.3 us (3%)
    all_to_all x1, blocking collectives, on_device(): got = lax.all_to_all(sent, 'ctx', 0, 0)  69.5 us
    all_to_all x2, waiting for transfers between devices, on_device(): lax.all_to_all(both.reshape(-1, outer, share), 'ctx', 1, 0, axis_index_gr...  56.8 us
    ppermute x2, waiting for transfers between devices, on_device(): other = lax.ppermute(sent.astype(jnp.bfloat16), 'ctx', swap)  34.9 us
    all_to_all x1, waiting for transfers between devices, on_device(): lax.all_to_all(projections, 'ctx', split_axis=2, concat_axis=1, tiled=True)  33.8 us
    ppermute x10, starting transfers between devices, exchange(): lax.ppermute(block, axis, [(i, (i + shift) % devices) for i in range(devi...  14.5 us
    unnamed x53, local copies, waits for them, and re-layouts  14.3 us
    ppermute x10, waiting for transfers between devices, exchange(): lax.ppermute(block, axis, [(i, (i + shift) % devices) for i in range(devi...  13.6 us
    pallas_call x1, Pallas kernels, run_backward(): pl.pallas_call(backward_kernel, grid=(width // lanes,), in_specs=[series,...  8.96 us
  transfers between devices with their start and end apart: 17, of which 8 were waited for; matrix products, arithmetic and copies ran while one was open for 13% of the time, Pallas kernels for 4%

profile of v4, /device:TPU:0, one launch (start us, length us, event | category | flops | bytes accessed | tf_op | source)
XLA Modules:
  0.0 337.4 jit_solution(3700830102022903850)
XLA Ops:
  11.6 3.0 collective-permute-done
  14.5 3.8 %collective-permute-done.1 = bf16[32,2048]{1,0:T(8,128)(2,1)S(1)} collective-permute-done((bf16[32,2048]{1,0:T(8,128)(2,1)S(1)}, bf16[32,2048]{1,0:T(8,128)(2,1)S(1)}, u32[]{:S(2)}, u32[]{:S(2)}) %collective-permute-start.1) | collective-permute-done | bytes 131104 | tf_op jit(solution)/shard_map/ppermute | solution.py:187
  20.4 4.7 %collective-permute-start.3 = (bf16[32,1024]{1,0:T(8,128)(2,1)S(1)}, bf16[32,1024]{1,0:T(8,128)(2,1)S(1)}, u32[]{:S(2)}, u32[]{:S(2)}) collective-permute-start(bf16[32,1024]{1,0:T(8,128)(2,1)S(1)} %get-tuple-element.43), channel_id=1, source_target_pairs={{0,28},{4,0},{8,4},{12,8},{16,12},{20,16},{24,20},{28,24},{1,29},{... | collective-permute-start | bytes 196616 | tf_op jit(solution)/shard_map/ppermute | solution.py:187
  25.6 3.0 collective-permute-start.6
  31.7 2.9 collective-permute-done.6
  34.5 4.0 %collective-permute-done.7 = bf16[32,1024]{1,0:T(8,128)(2,1)S(1)} collective-permute-done((bf16[32,1024]{1,0:T(8,128)(2,1)S(1)}, bf16[32,1024]{1,0:T(8,128)(2,1)S(1)}, u32[]{:S(2)}, u32[]{:S(2)}) %collective-permute-start.7) | collective-permute-done | bytes 65568 | tf_op jit(solution)/shard_map/ppermute | solution.py:187
  39.6 2.5 copy.50
  42.2 3.6 %all-to-all-start = ((bf16[3,128,2048]{1,0,2:T(4,128)(2,1)}), bf16[3,128,2048]{1,0,2:T(4,128)(2,1)S(1)}, u32[]{:S(2)}, u32[]{:S(2)}) async-start(bf16[3,128,2048]{1,0,2:T(4,128)(2,1)} %copy.50), calls=%async_computation | async-start | bytes 4194304 | tf_op jit(solution)/shard_map/all_to_all | solution.py:200
  45.8 6.4 %copy.53 = bf16[1024,2048]{0,1:T(8,128)(2,1)} copy(bf16[1024,2048]{1,0:T(8,128)(2,1)} %param.7) | data formatting | bytes 8388608 | tf_op args[1]
  54.0 4.7 %constant_dynamic-slice_fusion.6 = (bf16[1024,4,1,256]{0,3,2,1:T(8,128)(2,1)}, bf16[1024,4,1,256]{0,3,2,1:T(8,128)(2,1)}) fusion(bf16[1024,4,2,256]{0,3,2,1:T(8,128)(2,1)} %bitcast.127, s32[]{:T(128)S(6)} %select_n.70, s32[]{:T(128)S(6)} %select_n.71), kind=kLoop, calls=%fused_computation.88 | loop fusion | bytes 8388616 | tf_op jit(solution)/shard_map/jit(dynamic_index_in_dim)/dynamic_slice | solution.py:233
  58.7 33.8 %all-to-all-done = bf16[3,128,2048]{1,0,2:T(4,128)(2,1)S(1)} async-done(((bf16[3,128,2048]{1,0,2:T(4,128)(2,1)}), bf16[3,128,2048]{1,0,2:T(4,128)(2,1)S(1)}, u32[]{:S(2)}, u32[]{:S(2)}) %all-to-all-start) | async-done | bytes 1572896 | tf_op jit(solution)/shard_map/all_to_all | solution.py:200
  95.6 3.3 convolution_convert_fusion.1
  107.2 4.0 %shard_map.101 = (f32[128,8,256]{2,1,0:T(8,128)S(1)}, f32[16,8,256]{2,1,0:T(8,128)S(1)}) custom-call(f32[128,8,256]{2,1,0:T(8,128)S(1)} %bitcast.123, f32[16,1,256]{2,1,0:T(1,128)S(1)} %copy.55.decay_ref, f32[16,1,256]{2,1,0:T(1,128)S(1)} %broadcast_in_dim.16.jump_ref, f32[16,1,256]{2,1,0:T(1,128)S(1)} %broadcast_in_dim.17.res_ref), custom_call_target="tpu_custom_call" | custom-call | flops 25165824 | bytes 2097152 | tf_op jit(solution)/shard_map/pallas_call | solution.py:125
  112.7 34.9 %collective-permute-done.10 = bf16[512,1024]{1,0:T(8,128)(2,1)} collective-permute-done((bf16[512,1024]{1,0:T(8,128)(2,1)}, bf16[512,1024]{1,0:T(8,128)(2,1)}, u32[]{:S(2)}, u32[]{:S(2)}) %collective-permute-start.10) | collective-permute-done | bytes 1048608 | tf_op jit(solution)/shard_map/ppermute | solution.py:242
  147.6 4.6 %add_convert_fusion.2 = bf16[512,1024]{1,0:T(8,128)(2,1)} fusion(bf16[512,1024]{1,0:T(8,128)(2,1)} %collective-permute-done.10, bf16[1024,1024]{0,1:T(8,128)(2,1)} %bitcast.143, bf16[1024,1024]{1,0:T(8,128)(2,1)} %bitcast.158), kind=kOutput, calls=%fused_computation.10 | convolution fusion | flops 1075314688 | bytes 5242880 | tf_op jit(solution)/shard_map/dot_general | solution.py:243
  152.2 3.5 %add_convert_fusion.1 = bf16[512,1024]{1,0:T(8,128)(2,1)} fusion(bf16[512,1024]{1,0:T(8,128)(2,1)} %collective-permute-done.11, bf16[1024,1024]{0,1:T(8,128)(2,1)S(1)} %bitcast.144, bf16[1024,1024]{1,0:T(8,128)(2,1)S(1)} %bitcast.160), kind=kOutput, calls=%fused_computation.8 | convolution fusion | flops 1075314688 | bytes 5242880 | tf_op jit(solution)/shard_map/dot_general | solution.py:243
  158.6 3.7 %all-to-all-start.2 = ((bf16[1,512,4,256]{3,1,0,2:T(8,128)(2,1)}), bf16[1,512,4,256]{3,1,0,2:T(8,128)(2,1)S(1)}, u32[]{:S(2)}, u32[]{:S(2)}) async-start(bf16[1,512,4,256]{3,1,0,2:T(8,128)(2,1)} %copy.58), calls=%async_computation.2 | async-start | bytes 2097152 | tf_op jit(solution)/shard_map/all_to_all | solution.py:246
  162.3 2.6 broadcast_in_dim_reshape.6
  167.4 20.1 %all-to-all-done.2 = bf16[1,512,4,256]{3,1,0,2:T(8,128)(2,1)S(1)} async-done(((bf16[1,512,4,256]{3,1,0,2:T(8,128)(2,1)}), bf16[1,512,4,256]{3,1,0,2:T(8,128)(2,1)S(1)}, u32[]{:S(2)}, u32[]{:S(2)}) %all-to-all-start.2) | async-done | bytes 1048608 | tf_op jit(solution)/shard_map/all_to_all | solution.py:246
  187.4 4.2 %all-to-all-start.1 = ((bf16[1,512,4,256]{3,1,0,2:T(8,128)(2,1)}), bf16[1,512,4,256]{3,1,0,2:T(8,128)(2,1)}, u32[]{:S(2)}, u32[]{:S(2)}) async-start(bf16[1,512,4,256]{3,1,0,2:T(8,128)(2,1)} %copy.57), calls=%async_computation.1 | async-start | bytes 2097152 | tf_op jit(solution)/shard_map/all_to_all | solution.py:246
  193.8 36.8 %all-to-all-done.1 = bf16[1,512,4,256]{3,1,0,2:T(8,128)(2,1)} async-done(((bf16[1,512,4,256]{3,1,0,2:T(8,128)(2,1)}), bf16[1,512,4,256]{3,1,0,2:T(8,128)(2,1)}, u32[]{:S(2)}, u32[]{:S(2)}) %all-to-all-start.1) | async-done | bytes 1048608 | tf_op jit(solution)/shard_map/all_to_all | solution.py:246
  233.4 9.0 %shard_map.102 = (f32[128,8,256]{2,1,0:T(8,128)S(1)}, f32[16,1,256]{2,1,0:T(1,128)S(1)}, f32[16,1,256]{2,1,0:T(1,128)S(1)}) custom-call(f32[128,8,256]{2,1,0:T(8,128)S(1)} %bitcast.124, f32[128,8,256]{2,1,0:T(8,128)S(1)} %fusion.1.gl_ref, f32[16,1,256]{2,1,0:T(1,128)S(1)} %copy.55.decay_ref, f32[16,1,256]{2,1,0:T(1,128)S(1)} %broadcast_in_dim.16.jump_ref, ...), custom_call_target="tpu_custom_call" | custom-call | flops 50331648 | bytes 3145728 | tf_op jit(solution)/shard_map/pallas_call | solution.py:148
  249.2 69.5 %all_to_all.41 = bf16[8,480,256]{2,1,0:T(8,128)(2,1)S(1)} all-to-all(bf16[8,480,256]{2,1,0:T(8,128)(2,1)S(1)} %pad_maximum_fusion.1), channel_id=1, replica_groups=mesh['ctx'=8,'fsdp'=4] {'ctx'}, dimensions={0} | all-to-all | bytes 3932160 | tf_op jit(solution)/shard_map/all_to_all | solution.py:288
  322.3 8.3 %convolution_convert_fusion = bf16[1024,2048]{1,0:T(8,128)(2,1)} fusion(bf16[1024,1024]{1,0:T(8,128)(2,1)S(1)} %bitcast.161, bf16[1024,2048]{1,0:T(8,128)(2,1)} %all-gather.4.cloned.1.call-done), kind=kOutput, calls=%fused_computation | convolution fusion | flops 4297064448 | bytes 10485760 | tf_op jit(solution)/shard_map/dot_general | solution.py:254
  (125 shorter events, 45.9 us)
Async XLA Ops:
  7.2 88.4 %all-gather.6.cloned.1.call-start = ((), (), s32[]{:S(2)}) async-start(), calls=%async_computation.5 | async-start | bytes 2621440 | tf_op jit(solution)/shard_map/all_gather | solution.py:207
  8.3 6.2 %collective-permute-start = (bf16[32,2048]{1,0:T(8,128)(2,1)S(1)}, bf16[32,2048]{1,0:T(8,128)(2,1)S(1)}, u32[]{:S(2)}, u32[]{:S(2)}) collective-permute-start(bf16[32,2048]{1,0:T(8,128)(2,1)S(1)} %get-tuple-element.46), channel_id=1, source_target_pairs={{0,3},{1,0},{2,1},{3,2},{4,7},{5,4},{6,5},{7,6},{8,11},{9,8},{10,9... | collective-permute-start | bytes 393224 | tf_op jit(solution)/shard_map/ppermute | solution.py:187
  10.8 7.5 %collective-permute-start.1 = (bf16[32,2048]{1,0:T(8,128)(2,1)S(1)}, bf16[32,2048]{1,0:T(8,128)(2,1)S(1)}, u32[]{:S(2)}, u32[]{:S(2)}) collective-permute-start(bf16[32,2048]{1,0:T(8,128)(2,1)S(1)} %get-tuple-element.45), channel_id=1, source_target_pairs={{0,2},{1,3},{2,0},{3,1},{4,6},{5,7},{6,4},{7,5},{8,10},{9,11},{10,... | collective-permute-start | bytes 393224 | tf_op jit(solution)/shard_map/ppermute | solution.py:187
  11.4 6.9 %collective-permute-start.2 = (bf16[32,2048]{1,0:T(8,128)(2,1)S(1)}, bf16[32,2048]{1,0:T(8,128)(2,1)S(1)}, u32[]{:S(2)}, u32[]{:S(2)}) collective-permute-start(bf16[32,2048]{1,0:T(8,128)(2,1)S(1)} %get-tuple-element.44), channel_id=1, source_target_pairs={{0,1},{1,2},{2,3},{3,0},{4,5},{5,6},{6,7},{7,4},{8,9},{9,10},{10,1... | collective-permute-start | bytes 393224 | tf_op jit(solution)/shard_map/ppermute | solution.py:187
  20.3 19.3 %copy-start.8 = (bf16[3,128,2048]{2,1,0:T(8,128)(2,1)S(1)}, bf16[3,128,2048]{2,1,0:T(8,128)(2,1)}, u32[]{:S(2)}) copy-start(bf16[3,128,2048]{2,1,0:T(8,128)(2,1)} %param.8) | copy-start | bytes 4718596
  20.4 8.2 %collective-permute-start.3 = (bf16[32,1024]{1,0:T(8,128)(2,1)S(1)}, bf16[32,1024]{1,0:T(8,128)(2,1)S(1)}, u32[]{:S(2)}, u32[]{:S(2)}) collective-permute-start(bf16[32,1024]{1,0:T(8,128)(2,1)S(1)} %get-tuple-element.43), channel_id=1, source_target_pairs={{0,28},{4,0},{8,4},{12,8},{16,12},{20,16},{24,20},{28,24},{1,29},{... | collective-permute-start | bytes 196616 | tf_op jit(solution)/shard_map/ppermute | solution.py:187
  25.1 5.3 %collective-permute-start.4 = (bf16[32,1024]{1,0:T(8,128)(2,1)S(1)}, bf16[32,1024]{1,0:T(8,128)(2,1)S(1)}, u32[]{:S(2)}, u32[]{:S(2)}) collective-permute-start(bf16[32,1024]{1,0:T(8,128)(2,1)S(1)} %get-tuple-element.42), channel_id=1, source_target_pairs={{0,24},{4,28},{8,0},{12,4},{16,8},{20,12},{24,16},{28,20},{1,25},{... | collective-permute-start | bytes 196616 | tf_op jit(solution)/shard_map/ppermute | solution.py:187
  25.6 6.0 %collective-permute-start.5 = (bf16[32,1024]{1,0:T(8,128)(2,1)S(1)}, bf16[32,1024]{1,0:T(8,128)(2,1)S(1)}, u32[]{:S(2)}, u32[]{:S(2)}) collective-permute-start(bf16[32,1024]{1,0:T(8,128)(2,1)S(1)} %get-tuple-element.41), channel_id=1, source_target_pairs={{0,20},{4,24},{8,28},{12,0},{16,4},{20,8},{24,12},{28,16},{1,21},{... | collective-permute-start | bytes 196616 | tf_op jit(solution)/shard_map/ppermute | solution.py:187
  25.6 8.9 %collective-permute-start.6 = (bf16[32,1024]{1,0:T(8,128)(2,1)S(1)}, bf16[32,1024]{1,0:T(8,128)(2,1)S(1)}, u32[]{:S(2)}, u32[]{:S(2)}) collective-permute-start(bf16[32,1024]{1,0:T(8,128)(2,1)S(1)} %get-tuple-element.40), channel_id=1, source_target_pairs={{0,16},{4,20},{8,24},{12,28},{16,0},{20,4},{24,8},{28,12},{1,17},{... | collective-permute-start | bytes 196616 | tf_op jit(solution)/shard_map/ppermute | solution.py:187
  28.6 9.9 %collective-permute-start.7 = (bf16[32,1024]{1,0:T(8,128)(2,1)S(1)}, bf16[32,1024]{1,0:T(8,128)(2,1)S(1)}, u32[]{:S(2)}, u32[]{:S(2)}) collective-permute-start(bf16[32,1024]{1,0:T(8,128)(2,1)S(1)} %get-tuple-element.39), channel_id=1, source_target_pairs={{0,12},{4,16},{8,20},{12,24},{16,28},{20,0},{24,4},{28,8},{1,13},{... | collective-permute-start | bytes 196616 | tf_op jit(solution)/shard_map/ppermute | solution.py:187
  28.6 9.9 %collective-permute-start.8 = (bf16[32,1024]{1,0:T(8,128)(2,1)S(1)}, bf16[32,1024]{1,0:T(8,128)(2,1)S(1)}, u32[]{:S(2)}, u32[]{:S(2)}) collective-permute-start(bf16[32,1024]{1,0:T(8,128)(2,1)S(1)} %get-tuple-element.38), channel_id=1, source_target_pairs={{0,8},{4,12},{8,16},{12,20},{16,24},{20,28},{24,0},{28,4},{1,9},{5... | collective-permute-start | bytes 196616 | tf_op jit(solution)/shard_map/ppermute | solution.py:187
  30.4 8.1 %collective-permute-start.9 = (bf16[32,1024]{1,0:T(8,128)(2,1)S(1)}, bf16[32,1024]{1,0:T(8,128)(2,1)S(1)}, u32[]{:S(2)}, u32[]{:S(2)}) collective-permute-start(bf16[32,1024]{1,0:T(8,128)(2,1)S(1)} %get-tuple-element.37), channel_id=1, source_target_pairs={{0,4},{4,8},{8,12},{12,16},{16,20},{20,24},{24,28},{28,0},{1,5},{5... | collective-permute-start | bytes 196616 | tf_op jit(solution)/shard_map/ppermute | solution.py:187
  42.2 50.3 %all-to-all-start = ((bf16[3,128,2048]{1,0,2:T(4,128)(2,1)}), bf16[3,128,2048]{1,0,2:T(4,128)(2,1)S(1)}, u32[]{:S(2)}, u32[]{:S(2)}) async-start(bf16[3,128,2048]{1,0,2:T(4,128)(2,1)} %copy.50), calls=%async_computation | async-start | bytes 4194304 | tf_op jit(solution)/shard_map/all_to_all | solution.py:200
  95.6 3.4 copy-start.7
  101.3 50.9 %collective-permute-start.11 = (bf16[512,1024]{1,0:T(8,128)(2,1)S(1)}, bf16[512,1024]{1,0:T(8,128)(2,1)}, u32[]{:S(2)}, u32[]{:S(2)}) collective-permute-start(bf16[512,1024]{1,0:T(8,128)(2,1)S(1)} %convolution_convert_fusion.1), channel_id=1, source_target_pairs={{0,4},{4,0},{8,12},{12,8},{16,20},{20,16},{24,28},{28,24},{1,5},{5... | collective-permute-start | bytes 3145736 | tf_op jit(solution)/shard_map/ppermute | solution.py:242
  102.6 44.9 %collective-permute-start.10 = (bf16[512,1024]{1,0:T(8,128)(2,1)}, bf16[512,1024]{1,0:T(8,128)(2,1)}, u32[]{:S(2)}, u32[]{:S(2)}) collective-permute-start(bf16[512,1024]{1,0:T(8,128)(2,1)} %convolution_convert_fusion.2), channel_id=1, source_target_pairs={{0,4},{4,0},{8,12},{12,8},{16,20},{20,16},{24,28},{28,24},{1,5},{5... | collective-permute-start | bytes 3145736 | tf_op jit(solution)/shard_map/ppermute | solution.py:242
  105.3 6.3 %copy-start.2 = (f32[3,1024,256]{2,1,0:T(8,128)}, f32[3,1024,256]{2,1,0:T(8,128)S(1)}, u32[]{:S(2)}) copy-start(f32[3,1024,256]{2,1,0:T(8,128)S(1)} %multiply_add_fusion) | copy-start | bytes 9437188
  147.6 4.6 %copy-start.6 = (bf16[1024,4,1,256]{0,3,2,1:T(8,128)(2,1)S(1)}, bf16[1024,4,1,256]{0,3,2,1:T(8,128)(2,1)}, u32[]{:S(2)}) copy-start(bf16[1024,4,1,256]{0,3,2,1:T(8,128)(2,1)} %get-tuple-element.30) | copy-start | bytes 6291460
  147.6 4.6 %copy-start.10 = (bf16[8,128,1024]{2,1,0:T(8,128)(2,1)S(1)}, bf16[8,128,1024]{2,1,0:T(8,128)(2,1)}, u32[]{:S(2)}) copy-start(bf16[8,128,1024]{2,1,0:T(8,128)(2,1)} %all-gather.6.cloned.1.call-done) | copy-start | bytes 6291460
  158.6 28.8 %all-to-all-start.2 = ((bf16[1,512,4,256]{3,1,0,2:T(8,128)(2,1)}), bf16[1,512,4,256]{3,1,0,2:T(8,128)(2,1)S(1)}, u32[]{:S(2)}, u32[]{:S(2)}) async-start(bf16[1,512,4,256]{3,1,0,2:T(8,128)(2,1)} %copy.58), calls=%async_computation.2 | async-start | bytes 2097152 | tf_op jit(solution)/shard_map/all_to_all | solution.py:246
  187.4 4.3 %copy-start.5 = (bf16[1,512,4,256]{3,1,0,2:T(8,128)(2,1)}, bf16[1,512,4,256]{3,1,0,2:T(8,128)(2,1)S(1)}, u32[]{:S(2)}) copy-start(bf16[1,512,4,256]{3,1,0,2:T(8,128)(2,1)S(1)} %all-to-all-done.2) | copy-start | bytes 3145732
  187.4 43.2 %all-to-all-start.1 = ((bf16[1,512,4,256]{3,1,0,2:T(8,128)(2,1)}), bf16[1,512,4,256]{3,1,0,2:T(8,128)(2,1)}, u32[]{:S(2)}, u32[]{:S(2)}) async-start(bf16[1,512,4,256]{3,1,0,2:T(8,128)(2,1)} %copy.57), calls=%async_computation.1 | async-start | bytes 2097152 | tf_op jit(solution)/shard_map/all_to_all | solution.py:246
  191.7 130.6 %all-gather.4.cloned.1.call-start = ((), (), s32[]{:S(2)}) async-start(), calls=%async_computation.4 | async-start | bytes 4718592 | tf_op jit(solution)/shard_map/all_gather | solution.py:250
  318.7 3.5 %copy-start.11 = (bf16[8,128,1024]{2,1,0:T(8,128)(2,1)S(1)}, bf16[8,128,1024]{2,1,0:T(8,128)(2,1)}, u32[]{:S(2)}) copy-start(bf16[8,128,1024]{2,1,0:T(8,128)(2,1)} %all-gather.6.cloned.1.call-done) | copy-start | bytes 6291460
  (5 other events, 10.5 us)
Sparse Core Ops, SparseCore 0:
  39.8 19.9 all-gather.5
  194.5 116.0 all-gather.3
